TPU v7x, 32 devices: a whole 2x2x4 slice. The times are simulated.
32 devices in a mesh: gx: 8 (over z, x), gy: 4 (over y, core).
Axes of the slice: x: 2, y: 2, z: 4, core: 2. Of those that a mesh axis runs over, the one named last changes fastest.
Arguments:
- disp: float32 [2, 64, 4096], P(None, 'gx', 'gy'), may hold values from -0.2 to 0.2
- vel: float32 [2, 64, 4096], P(None, 'gx', 'gy'), may hold values from -1 to 1
- bonds: int32 [4, 64, 4096], P(None, 'gx', 'gy'), may hold values from 0 to 127, as said below
Outputs:
- new_disp: float32 [2, 64, 4096], P(None, 'gx', 'gy')
- new_vel: float32 [2, 64, 4096], P(None, 'gx', 'gy')
Inputs may be any that keep to these rules, and one draw needn't show every extreme that they name: `bonds`: bit j of word 0 is bit j of the table's word 0 (j < 3), bits 0 to 6 of words 1 to 3 likewise; word 0 is below 8 and no higher bits are set.
All inputs are finite; a program needn't handle non-finite values.
Results may differ from a plain program's by a relative error of at most 0.00002.
Values sent between devices are 32-bit elements; how exact they have to be, the bound alone decides.
A program may use at most 64 MiB of HBM per device.

v0:
```python
import math

import jax
import jax.numpy as jnp
from jax import lax
from jax.sharding import PartitionSpec as P

STEPS = 2


STIFFNESS = 40.0
DAMPING = 1.0
TIME_STEP = 0.05
SOFTENING = 0.0625
BOND_TABLE = [(0, c, 0, c - 1) for c in (1, 2, 3)] + [
    (r, c, r, c + 3) for r in (1, 2, 3) for c in (-3, -2, -1, 0, 1, 2, 3)
]
PACK_SHIFT = (0, 3, 10, 17)


def extended(block, sides, width):
    for axis, dim in sides:
        count = lax.axis_size(axis)
        forward = [(i, i + 1) for i in range(count - 1)]
        forward.append((count - 1, 0))
        backward = [(target, source) for source, target in forward]
        low = lax.ppermute(
            lax.slice_in_dim(block, block.shape[dim] - width, None, axis=dim), axis, forward
        )
        high = lax.ppermute(lax.slice_in_dim(block, 0, width, axis=dim), axis, backward)
        block = jnp.concatenate([low, block, high], axis=dim)
    return block


def passed_along(array, axis, by):
    devices = lax.axis_size(axis)
    return lax.ppermute(array, axis, [(i, (i + by) % devices) for i in range(devices)])


def bond_force(near_state, far_state, row_off, col_off, intact):
    length = math.sqrt(row_off * row_off + col_off * col_off)
    rest = math.sqrt(length * length + SOFTENING)
    along_x = row_off + far_state[0] - near_state[0]
    along_y = col_off + far_state[1] - near_state[1]
    stretched = jnp.sqrt(along_x * along_x + along_y * along_y + SOFTENING)
    strain = (stretched - rest) / length
    closing = (
        along_x * (far_state[2] - near_state[2]) + along_y * (far_state[3] - near_state[3])
    ) / (stretched * length)
    tension = intact * (STIFFNESS * strain + DAMPING * closing) / length
    return (tension * along_x / stretched, tension * along_y / stretched)


def intact_bits(word_array, bit):
    return jnp.bitwise_and(jnp.right_shift(word_array, bit), 1).astype(jnp.float32)


def twice_force(state, bonds, mask_box, row_count, col_count):
    padded_state = extended(state, (("gx", 1), ("gy", 2)), 3)
    own_state = padded_state[:, 3 : 3 + row_count, 3 : 3 + col_count]
    force_x = jnp.zeros((row_count, col_count), jnp.float32)
    force_y = jnp.zeros((row_count, col_count), jnp.float32)
    for row_off, col_off, word, bit in BOND_TABLE:
        far_state = padded_state[
            :, 3 + row_off : 3 + row_off + row_count, 3 + col_off : 3 + col_off + col_count
        ]
        pull_x, pull_y = bond_force(
            own_state, far_state, row_off, col_off, intact_bits(bonds[word], bit)
        )
        near_state = padded_state[
            :, 3 - row_off : 3 - row_off + row_count, 3 - col_off : 3 - col_off + col_count
        ]
        near_words = mask_box[
            3 - row_off : 3 - row_off + row_count, 3 - col_off : 3 - col_off + col_count
        ]
        push_x, push_y = bond_force(
            near_state, own_state, row_off, col_off, intact_bits(near_words, PACK_SHIFT[word] + bit)
        )
        force_x = force_x + pull_x - push_x
        force_y = force_y + pull_y - push_y
    return jnp.stack([force_x, force_y])


def per_device(disp, vel, bonds):
    row_count = disp.shape[1]
    col_count = disp.shape[2]
    packed = bonds[0] + bonds[1] * 8 + bonds[2] * 1024 + bonds[3] * 131072
    earlier = passed_along(packed[row_count - 3 :, :], "gx", 1)
    mask_box = extended(jnp.concatenate([earlier, packed], 0), (("gy", 1),), 3)

    def forces(state):
        return twice_force(state, bonds, mask_box, row_count, col_count)

    acceleration = forces(jnp.concatenate([disp, vel], 0))
    for step in range(STEPS):
        half_vel = vel + 0.5 * TIME_STEP * acceleration
        disp = disp + TIME_STEP * half_vel
        acceleration = forces(jnp.concatenate([disp, half_vel], 0))
        vel = half_vel + 0.5 * TIME_STEP * acceleration
    return (disp, vel)


def solution(mesh):
    in_specs = (P(None, "gx", "gy"), P(None, "gx", "gy"), P(None, "gx", "gy"))
    out_specs = (P(None, "gx", "gy"), P(None, "gx", "gy"))
    return jax.shard_map(
        per_device, mesh=mesh, in_specs=in_specs, out_specs=out_specs, check_vma=False
    )
```

profile of v0, /device:TPU:1, one launch (start us, length us, event | category | flops | bytes accessed | tf_op | source)
XLA Modules:
  0.0 60.5 jit_solution(6660888250079851601)
XLA Ops:
  1.5 2.1 %collective-permute-start.3 = (s32[3,1024]{1,0:T(4,128)S(1)}, s32[3,1024]{1,0:T(4,128)S(1)}, u32[]{:S(2)}, u32[]{:S(2)}) collective-permute-start(s32[3,1024]{1,0:T(4,128)S(1)} %slice_bitcast_fusion), channel_id=1, source_target_pairs={{0,4},{4,8},{8,12},{12,16},{16,20},{20,24},{24,28},{28,0},{1,5},{5... | collective-permute-start | bytes 36872 | tf_op jit(solution)/shard_map/ppermute | solution.py:37
  3.7 3.8 %collective-permute-start.1 = (f32[4,3,1024]{2,1,0:T(4,128)S(1)}, f32[4,3,1024]{2,1,0:T(4,128)S(1)}, u32[]{:S(2)}, u32[]{:S(2)}) collective-permute-start(f32[4,3,1024]{2,1,0:T(4,128)S(1)} %get-tuple-element.109), channel_id=1, source_target_pairs={{4,0},{8,4},{12,8},{16,12},{20,16},{24,20},{28,24},{0,28},{5,1},{9... | collective-permute-start | bytes 147464 | tf_op jit(solution)/shard_map/ppermute | solution.py:30
  8.0 1.4 %collective-permute-start.6 = (s32[11,3]{1,0:T(8,128)S(1)}, s32[11,3]{1,0:T(8,128)S(1)}, u32[]{:S(2)}, u32[]{:S(2)}) collective-permute-start(s32[11,3]{1,0:T(8,128)S(1)} %get-tuple-element.113), channel_id=1, source_target_pairs={{1,0},{2,1},{3,2},{0,3},{5,4},{6,5},{7,6},{4,7},{9,8},{10,9},{11,1... | collective-permute-start | bytes 404 | tf_op jit(solution)/shard_map/ppermute | solution.py:30
  9.4 1.4 %collective-permute-start.4 = (s32[11,3]{1,0:T(8,128)S(1)}, s32[11,3]{1,0:T(8,128)S(1)}, u32[]{:S(2)}, u32[]{:S(2)}) collective-permute-start(s32[11,3]{1,0:T(8,128)S(1)} %get-tuple-element.114), channel_id=1, source_target_pairs={{0,1},{1,2},{2,3},{3,0},{4,5},{5,6},{6,7},{7,4},{8,9},{9,10},{10,1... | collective-permute-start | bytes 404 | tf_op jit(solution)/shard_map/ppermute | solution.py:27
  10.8 1.5 %collective-permute-done.6 = s32[11,3]{1,0:T(8,128)S(1)} collective-permute-done((s32[11,3]{1,0:T(8,128)S(1)}, s32[11,3]{1,0:T(8,128)S(1)}, u32[]{:S(2)}, u32[]{:S(2)}) %collective-permute-start.6) | collective-permute-done | bytes 164 | tf_op jit(solution)/shard_map/ppermute | solution.py:30
  12.4 4.5 %collective-permute-done = f32[4,3,1024]{2,1,0:T(4,128)S(1)} collective-permute-done((f32[4,3,1024]{2,1,0:T(4,128)S(1)}, f32[4,3,1024]{2,1,0:T(4,128)S(1)}, u32[]{:S(2)}, u32[]{:S(2)}) %collective-permute-start) | collective-permute-done | bytes 49184 | tf_op jit(solution)/shard_map/ppermute | solution.py:27
  17.0 1.4 %collective-permute-start.5 = (f32[4,14,3]{2,1,0:T(8,128)S(1)}, f32[4,14,3]{2,1,0:T(8,128)S(1)}, u32[]{:S(2)}, u32[]{:S(2)}) collective-permute-start(f32[4,14,3]{2,1,0:T(8,128)S(1)} %get-tuple-element.99), channel_id=1, source_target_pairs={{0,1},{1,2},{2,3},{3,0},{4,5},{5,6},{6,7},{7,4},{8,9},{9,10},{10,1... | collective-permute-start | bytes 2024 | tf_op jit(solution)/shard_map/ppermute | solution.py:27
  19.4 2.3 %collective-permute-done.2 = f32[4,14,3]{2,1,0:T(8,128)S(1)} collective-permute-done((f32[4,14,3]{2,1,0:T(8,128)S(1)}, f32[4,14,3]{2,1,0:T(8,128)S(1)}, u32[]{:S(2)}, u32[]{:S(2)}) %collective-permute-start.2) | collective-permute-done | bytes 704 | tf_op jit(solution)/shard_map/ppermute | solution.py:30
  21.9 3.0 %subtract_bitcast_fusion.5 = (f32[1,8,1024]{2,1,0:T(8,128)S(1)}, f32[8,1024]{1,0:T(8,128)S(1)}, f32[8,1024]{1,0:T(8,128)S(1)}, f32[8,1024]{1,0:T(8,128)S(1)}, f3...) fusion(f32[8,1024]{1,0:T(8,128)S(1)} %get-tuple-element.86, ...), kind=kLoop, calls=%fused_computation.2557 | loop fusion | flops 9281536 | bytes 8728576 | tf_op jit(solution)/shard_map/stack | solution.py:81
  24.9 1.3 %subtract_bitcast_fusion.4 = f32[1,8,1024]{2,1,0:T(8,128)S(1)} fusion(f32[8,1024]{1,0:T(8,128)S(1)} %get-tuple-element.76, f32[8,1024]{1,0:T(8,128)S(1)} %get-tuple-element.75, f32[8,1024]{1,0:T(8,128)S(1)} %get-tuple-element.74, f32[8,1024]{1,0:T(8,128)S(1)} %get-tuple-element.73, f32[8,1024]{1,0:T(8,128)S(1)} %get-tuple-element.72, ...), kind=kLoop, calls=%fused_computation.2556 | loop fusion | flops 3825664 | bytes 4816896 | tf_op jit(solution)/shard_map/stack | solution.py:81
  26.3 4.1 %collective-permute-start.8 = (f32[4,3,1024]{2,1,0:T(4,128)S(1)}, f32[4,3,1024]{2,1,0:T(4,128)S(1)}, u32[]{:S(2)}, u32[]{:S(2)}) collective-permute-start(f32[4,3,1024]{2,1,0:T(4,128)S(1)} %get-tuple-element.108), channel_id=1, source_target_pairs={{4,0},{8,4},{12,8},{16,12},{20,16},{24,20},{28,24},{0,28},{5,1},{9... | collective-permute-start | bytes 147464 | tf_op jit(solution)/shard_map/ppermute | solution.py:30
  30.5 1.9 %collective-permute-done.7 = f32[4,3,1024]{2,1,0:T(4,128)S(1)} collective-permute-done((f32[4,3,1024]{2,1,0:T(4,128)S(1)}, f32[4,3,1024]{2,1,0:T(4,128)S(1)}, u32[]{:S(2)}, u32[]{:S(2)}) %collective-permute-start.7) | collective-permute-done | bytes 49184 | tf_op jit(solution)/shard_map/ppermute | solution.py:27
  32.5 1.5 %collective-permute-start.10 = (f32[4,14,3]{2,1,0:T(8,128)S(1)}, f32[4,14,3]{2,1,0:T(8,128)S(1)}, u32[]{:S(2)}, u32[]{:S(2)}) collective-permute-start(f32[4,14,3]{2,1,0:T(8,128)S(1)} %get-tuple-element.95), channel_id=1, source_target_pairs={{0,1},{1,2},{2,3},{3,0},{4,5},{5,6},{6,7},{7,4},{8,9},{9,10},{10,1... | collective-permute-start | bytes 2024 | tf_op jit(solution)/shard_map/ppermute | solution.py:27
  34.0 1.0 %collective-permute-done.10 = f32[4,14,3]{2,1,0:T(8,128)S(1)} collective-permute-done((f32[4,14,3]{2,1,0:T(8,128)S(1)}, f32[4,14,3]{2,1,0:T(8,128)S(1)}, u32[]{:S(2)}, u32[]{:S(2)}) %collective-permute-start.10) | collective-permute-done | bytes 704 | tf_op jit(solution)/shard_map/ppermute | solution.py:27
  35.0 2.3 %collective-permute-done.9 = f32[4,14,3]{2,1,0:T(8,128)S(1)} collective-permute-done((f32[4,14,3]{2,1,0:T(8,128)S(1)}, f32[4,14,3]{2,1,0:T(8,128)S(1)}, u32[]{:S(2)}, u32[]{:S(2)}) %collective-permute-start.9) | collective-permute-done | bytes 704 | tf_op jit(solution)/shard_map/ppermute | solution.py:30
  37.5 2.9 %subtract_bitcast_fusion.3 = (f32[1,8,1024]{2,1,0:T(8,128)S(1)}, f32[8,1024]{1,0:T(8,128)S(1)}, f32[8,1024]{1,0:T(8,128)S(1)}, f32[8,1024]{1,0:T(8,128)S(1)}, f3...) fusion(f32[4,14,1027]{2,1,0:T(8,128)S(1)} %get-tuple-element.94, ...), kind=kLoop, calls=%fused_computation.2507 | loop fusion | flops 9805824 | bytes 7647232 | tf_op jit(solution)/shard_map/stack | solution.py:81
  40.4 2.6 %subtract_bitcast_fusion.2 = f32[1,8,1024]{2,1,0:T(8,128)S(1)} fusion(f32[8,1024]{1,0:T(8,128)S(1)} %get-tuple-element.25, f32[8,1024]{1,0:T(8,128)S(1)} %get-tuple-element.24, f32[8,1024]{1,0:T(8,128)S(1)} %get-tuple-element.23, f32[8,1024]{1,0:T(8,128)S(1)} %get-tuple-element.22, f32[8,1024]{1,0:T(8,128)S(1)} %get-tuple-element.21, ...), kind=kLoop, calls=%fused_computation.2506 | loop fusion | flops 8601600 | bytes 6815744 | tf_op jit(solution)/shard_map/stack | solution.py:81
  43.1 4.2 %collective-permute-start.12 = (f32[4,3,1024]{2,1,0:T(4,128)S(1)}, f32[4,3,1024]{2,1,0:T(4,128)S(1)}, u32[]{:S(2)}, u32[]{:S(2)}) collective-permute-start(f32[4,3,1024]{2,1,0:T(4,128)S(1)} %get-tuple-element.104), channel_id=1, source_target_pairs={{4,0},{8,4},{12,8},{16,12},{20,16},{24,20},{28,24},{0,28},{5,1},{9... | collective-permute-start | bytes 147464 | tf_op jit(solution)/shard_map/ppermute | solution.py:30
  47.3 1.8 %collective-permute-done.11 = f32[4,3,1024]{2,1,0:T(4,128)S(1)} collective-permute-done((f32[4,3,1024]{2,1,0:T(4,128)S(1)}, f32[4,3,1024]{2,1,0:T(4,128)S(1)}, u32[]{:S(2)}, u32[]{:S(2)}) %collective-permute-start.11) | collective-permute-done | bytes 49184 | tf_op jit(solution)/shard_map/ppermute | solution.py:27
  49.2 1.6 %collective-permute-start.14 = (f32[4,14,3]{2,1,0:T(8,128)S(1)}, f32[4,14,3]{2,1,0:T(8,128)S(1)}, u32[]{:S(2)}, u32[]{:S(2)}) collective-permute-start(f32[4,14,3]{2,1,0:T(8,128)S(1)} %get-tuple-element.91), channel_id=1, source_target_pairs={{0,1},{1,2},{2,3},{3,0},{4,5},{5,6},{6,7},{7,4},{8,9},{9,10},{10,1... | collective-permute-start | bytes 2024 | tf_op jit(solution)/shard_map/ppermute | solution.py:27
  50.9 1.0 %collective-permute-done.14 = f32[4,14,3]{2,1,0:T(8,128)S(1)} collective-permute-done((f32[4,14,3]{2,1,0:T(8,128)S(1)}, f32[4,14,3]{2,1,0:T(8,128)S(1)}, u32[]{:S(2)}, u32[]{:S(2)}) %collective-permute-start.14) | collective-permute-done | bytes 704 | tf_op jit(solution)/shard_map/ppermute | solution.py:27
  51.8 2.3 %collective-permute-done.13 = f32[4,14,3]{2,1,0:T(8,128)S(1)} collective-permute-done((f32[4,14,3]{2,1,0:T(8,128)S(1)}, f32[4,14,3]{2,1,0:T(8,128)S(1)}, u32[]{:S(2)}, u32[]{:S(2)}) %collective-permute-start.13) | collective-permute-done | bytes 704 | tf_op jit(solution)/shard_map/ppermute | solution.py:30
  54.4 2.9 %subtract_bitcast_fusion.1 = (f32[1,8,1024]{2,1,0:T(8,128)S(1)}, f32[8,1024]{1,0:T(8,128)S(1)}, f32[8,1024]{1,0:T(8,128)S(1)}, f32[8,1024]{1,0:T(8,128)S(1)}, f3...) fusion(f32[4,14,1027]{2,1,0:T(8,128)S(1)} %get-tuple-element.90, ...), kind=kLoop, calls=%fused_computation.2457 | loop fusion | flops 9805824 | bytes 7647232 | tf_op jit(solution)/shard_map/stack | solution.py:81
  57.2 2.6 %subtract_bitcast_fusion = f32[1,8,1024]{2,1,0:T(8,128)S(1)} fusion(f32[8,1024]{1,0:T(8,128)S(1)} %get-tuple-element.12, f32[8,1024]{1,0:T(8,128)S(1)} %get-tuple-element.11, f32[8,1024]{1,0:T(8,128)S(1)} %get-tuple-element.10, f32[8,1024]{1,0:T(8,128)S(1)} %get-tuple-element.9, f32[8,1024]{1,0:T(8,128)S(1)} %get-tuple-element.8, ...), kind=kLoop, calls=%fused_computation.2456 | loop fusion | flops 8601600 | bytes 6815744 | tf_op jit(solution)/shard_map/stack | solution.py:81
  (45 shorter events, 4.3 us)
Async XLA Ops:
  0.6 3.0 %copy-start.1 = (f32[2,8,1024]{2,1,0:T(8,128)S(1)}, f32[2,8,1024]{2,1,0:T(8,128)}, u32[]{:S(2)}) copy-start(f32[2,8,1024]{2,1,0:T(8,128)} %param.3) | copy-start | bytes 196612
  1.5 2.1 %copy-start.2 = (f32[2,8,1024]{2,1,0:T(8,128)S(1)}, f32[2,8,1024]{2,1,0:T(8,128)}, u32[]{:S(2)}) copy-start(f32[2,8,1024]{2,1,0:T(8,128)} %param.4) | copy-start | bytes 196612
  1.5 6.4 %collective-permute-start.3 = (s32[3,1024]{1,0:T(4,128)S(1)}, s32[3,1024]{1,0:T(4,128)S(1)}, u32[]{:S(2)}, u32[]{:S(2)}) collective-permute-start(s32[3,1024]{1,0:T(4,128)S(1)} %slice_bitcast_fusion), channel_id=1, source_target_pairs={{0,4},{4,8},{8,12},{12,16},{16,20},{20,24},{24,28},{28,0},{1,5},{5... | collective-permute-start | bytes 36872 | tf_op jit(solution)/shard_map/ppermute | solution.py:37
  3.7 3.9 %copy-start = (s32[4,8,1024]{2,1,0:T(8,128)S(1)}, s32[4,8,1024]{2,1,0:T(8,128)}, u32[]{:S(2)}) copy-start(s32[4,8,1024]{2,1,0:T(8,128)} %param.5) | copy-start | bytes 393220
  3.7 8.7 %collective-permute-start.1 = (f32[4,3,1024]{2,1,0:T(4,128)S(1)}, f32[4,3,1024]{2,1,0:T(4,128)S(1)}, u32[]{:S(2)}, u32[]{:S(2)}) collective-permute-start(f32[4,3,1024]{2,1,0:T(4,128)S(1)} %get-tuple-element.109), channel_id=1, source_target_pairs={{4,0},{8,4},{12,8},{16,12},{20,16},{24,20},{28,24},{0,28},{5,1},{9... | collective-permute-start | bytes 147464 | tf_op jit(solution)/shard_map/ppermute | solution.py:30
  8.0 4.3 %collective-permute-start.6 = (s32[11,3]{1,0:T(8,128)S(1)}, s32[11,3]{1,0:T(8,128)S(1)}, u32[]{:S(2)}, u32[]{:S(2)}) collective-permute-start(s32[11,3]{1,0:T(8,128)S(1)} %get-tuple-element.113), channel_id=1, source_target_pairs={{1,0},{2,1},{3,2},{0,3},{5,4},{6,5},{7,6},{4,7},{9,8},{10,9},{11,1... | collective-permute-start | bytes 404 | tf_op jit(solution)/shard_map/ppermute | solution.py:30
  9.4 2.9 %collective-permute-start.4 = (s32[11,3]{1,0:T(8,128)S(1)}, s32[11,3]{1,0:T(8,128)S(1)}, u32[]{:S(2)}, u32[]{:S(2)}) collective-permute-start(s32[11,3]{1,0:T(8,128)S(1)} %get-tuple-element.114), channel_id=1, source_target_pairs={{0,1},{1,2},{2,3},{3,0},{4,5},{5,6},{6,7},{7,4},{8,9},{9,10},{10,1... | collective-permute-start | bytes 404 | tf_op jit(solution)/shard_map/ppermute | solution.py:27
  10.8 6.1 %collective-permute-start = (f32[4,3,1024]{2,1,0:T(4,128)S(1)}, f32[4,3,1024]{2,1,0:T(4,128)S(1)}, u32[]{:S(2)}, u32[]{:S(2)}) collective-permute-start(f32[4,3,1024]{2,1,0:T(4,128)S(1)} %get-tuple-element.110), channel_id=1, source_target_pairs={{0,4},{4,8},{8,12},{12,16},{16,20},{20,24},{24,28},{28,0},{1,5},{5... | collective-permute-start | bytes 147464 | tf_op jit(solution)/shard_map/ppermute | solution.py:27
  17.0 2.4 %collective-permute-start.5 = (f32[4,14,3]{2,1,0:T(8,128)S(1)}, f32[4,14,3]{2,1,0:T(8,128)S(1)}, u32[]{:S(2)}, u32[]{:S(2)}) collective-permute-start(f32[4,14,3]{2,1,0:T(8,128)S(1)} %get-tuple-element.99), channel_id=1, source_target_pairs={{0,1},{1,2},{2,3},{3,0},{4,5},{5,6},{6,7},{7,4},{8,9},{9,10},{10,1... | collective-permute-start | bytes 2024 | tf_op jit(solution)/shard_map/ppermute | solution.py:27
  18.3 3.3 %collective-permute-start.2 = (f32[4,14,3]{2,1,0:T(8,128)S(1)}, f32[4,14,3]{2,1,0:T(8,128)S(1)}, u32[]{:S(2)}, u32[]{:S(2)}) collective-permute-start(f32[4,14,3]{2,1,0:T(8,128)S(1)} %get-tuple-element.100), channel_id=1, source_target_pairs={{1,0},{2,1},{3,2},{0,3},{5,4},{6,5},{7,6},{4,7},{9,8},{10,9},{11,1... | collective-permute-start | bytes 2024 | tf_op jit(solution)/shard_map/ppermute | solution.py:30
  26.3 6.1 %collective-permute-start.7 = (f32[4,3,1024]{2,1,0:T(4,128)S(1)}, f32[4,3,1024]{2,1,0:T(4,128)S(1)}, u32[]{:S(2)}, u32[]{:S(2)}) collective-permute-start(f32[4,3,1024]{2,1,0:T(4,128)S(1)} %get-tuple-element.107), channel_id=1, source_target_pairs={{0,4},{4,8},{8,12},{12,16},{16,20},{20,24},{24,28},{28,0},{1,5},{5... | collective-permute-start | bytes 147464 | tf_op jit(solution)/shard_map/ppermute | solution.py:27
  26.3 6.0 %collective-permute-start.8 = (f32[4,3,1024]{2,1,0:T(4,128)S(1)}, f32[4,3,1024]{2,1,0:T(4,128)S(1)}, u32[]{:S(2)}, u32[]{:S(2)}) collective-permute-start(f32[4,3,1024]{2,1,0:T(4,128)S(1)} %get-tuple-element.108), channel_id=1, source_target_pairs={{4,0},{8,4},{12,8},{16,12},{20,16},{24,20},{28,24},{0,28},{5,1},{9... | collective-permute-start | bytes 147464 | tf_op jit(solution)/shard_map/ppermute | solution.py:30
  32.5 2.5 %collective-permute-start.10 = (f32[4,14,3]{2,1,0:T(8,128)S(1)}, f32[4,14,3]{2,1,0:T(8,128)S(1)}, u32[]{:S(2)}, u32[]{:S(2)}) collective-permute-start(f32[4,14,3]{2,1,0:T(8,128)S(1)} %get-tuple-element.95), channel_id=1, source_target_pairs={{0,1},{1,2},{2,3},{3,0},{4,5},{5,6},{6,7},{7,4},{8,9},{9,10},{10,1... | collective-permute-start | bytes 2024 | tf_op jit(solution)/shard_map/ppermute | solution.py:27
  34.0 3.3 %collective-permute-start.9 = (f32[4,14,3]{2,1,0:T(8,128)S(1)}, f32[4,14,3]{2,1,0:T(8,128)S(1)}, u32[]{:S(2)}, u32[]{:S(2)}) collective-permute-start(f32[4,14,3]{2,1,0:T(8,128)S(1)} %get-tuple-element.96), channel_id=1, source_target_pairs={{1,0},{2,1},{3,2},{0,3},{5,4},{6,5},{7,6},{4,7},{9,8},{10,9},{11,1... | collective-permute-start | bytes 2024 | tf_op jit(solution)/shard_map/ppermute | solution.py:30
  43.0 14.2 %copy-start.3 = (f32[2,8,1024]{2,1,0:T(8,128)}, f32[2,8,1024]{2,1,0:T(8,128)S(1)}, u32[]{:S(2)}) copy-start(f32[2,8,1024]{2,1,0:T(8,128)S(1)} %get-tuple-element.13) | copy-start | bytes 196612
  43.0 6.1 %collective-permute-start.11 = (f32[4,3,1024]{2,1,0:T(4,128)S(1)}, f32[4,3,1024]{2,1,0:T(4,128)S(1)}, u32[]{:S(2)}, u32[]{:S(2)}) collective-permute-start(f32[4,3,1024]{2,1,0:T(4,128)S(1)} %get-tuple-element.103), channel_id=1, source_target_pairs={{0,4},{4,8},{8,12},{12,16},{16,20},{20,24},{24,28},{28,0},{1,5},{5... | collective-permute-start | bytes 147464 | tf_op jit(solution)/shard_map/ppermute | solution.py:27
  43.1 6.0 %collective-permute-start.12 = (f32[4,3,1024]{2,1,0:T(4,128)S(1)}, f32[4,3,1024]{2,1,0:T(4,128)S(1)}, u32[]{:S(2)}, u32[]{:S(2)}) collective-permute-start(f32[4,3,1024]{2,1,0:T(4,128)S(1)} %get-tuple-element.104), channel_id=1, source_target_pairs={{4,0},{8,4},{12,8},{16,12},{20,16},{24,20},{28,24},{0,28},{5,1},{9... | collective-permute-start | bytes 147464 | tf_op jit(solution)/shard_map/ppermute | solution.py:30
  49.2 2.6 %collective-permute-start.14 = (f32[4,14,3]{2,1,0:T(8,128)S(1)}, f32[4,14,3]{2,1,0:T(8,128)S(1)}, u32[]{:S(2)}, u32[]{:S(2)}) collective-permute-start(f32[4,14,3]{2,1,0:T(8,128)S(1)} %get-tuple-element.91), channel_id=1, source_target_pairs={{0,1},{1,2},{2,3},{3,0},{4,5},{5,6},{6,7},{7,4},{8,9},{9,10},{10,1... | collective-permute-start | bytes 2024 | tf_op jit(solution)/shard_map/ppermute | solution.py:27
  50.8 3.3 %collective-permute-start.13 = (f32[4,14,3]{2,1,0:T(8,128)S(1)}, f32[4,14,3]{2,1,0:T(8,128)S(1)}, u32[]{:S(2)}, u32[]{:S(2)}) collective-permute-start(f32[4,14,3]{2,1,0:T(8,128)S(1)} %get-tuple-element.92), channel_id=1, source_target_pairs={{1,0},{2,1},{3,2},{0,3},{5,4},{6,5},{7,6},{4,7},{9,8},{10,9},{11,1... | collective-permute-start | bytes 2024 | tf_op jit(solution)/shard_map/ppermute | solution.py:30
where the time goes:
time: 60.6 us; the launch traced here: 60.5 us
  starting transfers between devices  21.7 us (36%)
  waiting for transfers between devices  19.6 us (32%)
  other arithmetic  18.2 us (30%)
  between operations  0.89 us (1%)
    another operation x6, other arithmetic, twice_force(): return jnp.stack([force_x, force_y])  15.1 us
    ppermute x7, starting transfers between devices, extended(): lax.ppermute(lax.slice_in_dim(block, 0, width, axis=dim), axis, backward)  13.6 us
    ppermute x7, waiting for transfers between devices, extended(): lax.ppermute(lax.slice_in_dim(block, block.shape[dim] - width, None, axis...  10.8 us
    ppermute x7, waiting for transfers between devices, extended(): lax.ppermute(lax.slice_in_dim(block, 0, width, axis=dim), axis, backward)  8.48 us
    ppermute x7, starting transfers between devices, extended(): lax.ppermute(lax.slice_in_dim(block, block.shape[dim] - width, None, axis...  5.94 us
    ppermute x1, starting transfers between devices, passed_along(): lax.ppermute(array, axis, [(i, (i + by) % devices) for i in range(devices)])  2.09 us
  transfers between devices with their start and end apart: 15, of which 11 were waited for; matrix products, arithmetic and copies ran while one was open for 1% of the time, Pallas kernels for 0%

commit v1 on v0

v1 whole, which is shorter than its diff:
```python
import functools
import math

import jax
import jax.numpy as jnp
from jax import lax
from jax.experimental import pallas as pl
from jax.experimental.pallas import tpu as pltpu
from jax.sharding import PartitionSpec as P

STEPS = 2
STIFFNESS = 40.0
DAMPING = 1.0
TIME_STEP = 0.05
SOFTENING = 0.0625
REACH = 3
LANES = 128
GROUP = 2
PACK = (1, 8, 1024, 131072)
PACK_SHIFT = (0, 3, 10, 17)
MESH = pl.DeviceIdType.MESH
SHIFTS = tuple(range(-REACH, REACH + 1))


def bond_bit(a, b):
    return b - 1 if a == 0 else PACK_SHIFT[a] + b + REACH


OFFSETS = [(a, b) for a in SHIFTS for b in SHIFTS if (a, b) != (0, 0)]


def in_table(a, b):
    return a > 0 or (a == 0 and b > 0)


def shifted(x, low, high, b, segment, lane):
    segments = x.shape[0]
    if b > 0:
        after = jnp.where(segment == segments - 1, high, pltpu.roll(x, segments - 1, 0))
        return pltpu.roll(jnp.where(lane < b, after, x), LANES - b, 1)
    before = jnp.where(segment == 0, low, pltpu.roll(x, 1, 0))
    return pltpu.roll(jnp.where(lane >= LANES + b, before, x), -b, 1)


def kernel(
    disp_ref, vel_ref, bonds_ref, disp_out, vel_out,
    state, far, half, packed, masks, bond_rows, edge_out, edges_out,
    rows_in, row_bonds_in, edge_in, rows_next, edges_next, send, recv,
):
    rows = disp_ref.shape[1]
    segments = disp_ref.shape[2] // LANES
    gx, gy = lax.axis_index("gx"), lax.axis_index("gy")
    nx, ny = lax.axis_size("gx"), lax.axis_size("gy")
    gx_at = {-1: lax.rem(gx + nx - 1, nx), 0: gx, 1: lax.rem(gx + 1, nx)}
    gy_at = {-1: lax.rem(gy + ny - 1, ny), 0: gy, 1: lax.rem(gy + 1, ny)}
    around = [(x, y) for x in (-1, 0, 1) for y in (-1, 0, 1) if (x, y) != (0, 0)]

    barrier = pltpu.get_barrier_semaphore()
    for x, y in around:
        pl.semaphore_signal(
            barrier, inc=1, device_id=(gx_at[x], gy_at[y]), device_id_type=MESH
        )

    def by_segments(block):
        return block.reshape(rows, segments, LANES)

    last = (segments - 1) * LANES
    for f in range(2):
        for source, plane in ((disp_ref, f), (vel_ref, 2 + f)):
            state[plane] = by_segments(source[f])
            edge_out[0, plane] = source[f, :, 0:LANES]
            edge_out[1, plane] = source[f, :, last : last + LANES]
    words = []
    for w in range(4):
        word = bonds_ref[w].astype(jnp.float32)
        edge_out[0, 4 + w] = word[:, 0:LANES]
        edge_out[1, 4 + w] = word[:, last : last + LANES]
        words.append(by_segments(word))
    slot = 0
    row_bond_slots = {}
    for a in range(1, REACH + 1):
        for r in range(rows - a, rows):
            bond_rows[slot] = words[a][r]
            row_bond_slots[(a, r - rows)] = slot
            slot += 1
    own_packed = words[0] * PACK[0] + words[1] * PACK[1] + words[2] * PACK[2] + words[3] * PACK[3]
    packed[REACH, REACH : REACH + rows] = own_packed.astype(jnp.int32)

    def copy(phase, index, src, dst, x, y):
        return pltpu.make_async_remote_copy(
            src_ref=src, dst_ref=dst, send_sem=send.at[phase, index],
            recv_sem=recv.at[phase, index], device_id=(gx_at[x], gy_at[y]), device_id_type=MESH,
        )

    def copies(phase):
        if phase == 0:
            row_src, row_dst = state, rows_in
        else:
            row_src, row_dst = half.at[phase - 1], rows_next.at[phase - 1]
        out = {
            "down": copy(
                phase, 0, row_src.at[:, rows - REACH : rows], row_dst.at[0], 1, 0
            ),
            "up": copy(phase, 1, row_src.at[:, 0:REACH], row_dst.at[1], -1, 0),
        }
        if phase == 0:
            out["bonds"] = copy(phase, 2, bond_rows, row_bonds_in, 1, 0)
        index = 3
        for side in (0, 1):
            for slot, x in enumerate((1, 0, -1)):
                if phase == 0:
                    planes = 4 if x < 0 else 8
                    src = edge_out.at[side, 0:planes]
                    dst = edge_in.at[1 - side, slot, 0:planes]
                else:
                    src = edges_out.at[phase - 1, side]
                    dst = edges_next.at[phase - 1, 1 - side, slot]
                out[(side, x)] = copy(phase, index, src, dst, x, 2 * side - 1)
                index += 1
        return out

    pl.semaphore_wait(barrier, len(around))
    sent = [copies(0)]
    for c in sent[0].values():
        c.start()

    segment = lax.broadcasted_iota(jnp.int32, (segments, LANES), 0)
    lane = lax.broadcasted_iota(jnp.int32, (segments, LANES), 1)

    def edge_row(r):
        if r < REACH:
            return 0, rows - REACH + r
        if r < REACH + rows:
            return 1, r - REACH
        return 2, r - REACH - rows

    def wait_mid(phase):
        for side in (0, 1):
            sent[phase][(side, 0)].wait_recv()

    def wait_rest(phase):
        for key, c in sent[phase].items():
            if key not in ((0, 0), (1, 0)):
                c.wait_recv()

    def place(plane, r, x, low, high, phase):
        for b in SHIFTS:
            value = x if b == 0 else shifted(x, low, high, b, segment, lane)
            if phase == 0:
                far[plane, b + REACH, r] = value + b if plane == 1 and b else value
            else:
                far[2 + plane, b + REACH, r] = value
                far[plane, b + REACH, r] += TIME_STEP * value

    def place_rows(phase, wanted):
        for r in wanted:
            slot, e = edge_row(r)
            for plane in range(4 if phase == 0 else 2):
                if phase == 0:
                    row_from, edge_from = rows_in, edge_in
                    own = state[plane, r - REACH] if slot == 1 else None
                else:
                    row_from, edge_from = rows_next.at[phase - 1], edges_next.at[phase - 1]
                    own = half[phase - 1, plane, r - REACH] if slot == 1 else None
                if slot == 0:
                    own = row_from[0, plane, r]
                elif slot == 2:
                    own = row_from[1, plane, r - REACH - rows]
                low = edge_from[0, slot, plane, e : e + 1, :]
                high = edge_from[1, slot, plane, e : e + 1, :]
                place(plane, r, own, low, high, phase)

    def place_packed(wanted):
        for r in wanted:
            slot, e = edge_row(r)
            if slot == 0:
                x = jnp.zeros((segments, LANES), jnp.float32)
                for a in range(1, REACH + 1):
                    if (a, r - REACH) in row_bond_slots:
                        x = x + row_bonds_in[row_bond_slots[(a, r - REACH)]] * PACK[a]
                x = x.astype(jnp.int32)
                packed[REACH, r] = x
            else:
                x = packed[REACH, r]
            outer = []
            for side in (0, 1):
                value = edge_in[side, slot, 4, e : e + 1, :]
                for w in range(1, 4):
                    value = value + edge_in[side, slot, 4 + w, e : e + 1, :] * PACK[w]
                outer.append(value.astype(jnp.int32))
            for b in SHIFTS:
                if b:
                    packed[b + REACH, r] = shifted(x, outer[0], outer[1], b, segment, lane)

    def set_masks(index, a, b, first, count):
        scale = 1.0 / (a * a + b * b)
        if in_table(a, b):
            word = packed[REACH, first + REACH : first + REACH + count]
            bit = bond_bit(a, b)
        else:
            word = packed[b + REACH, first + REACH + a : first + REACH + a + count]
            bit = bond_bit(-a, -b)
        masks[index, first : first + count] = jnp.where(
            jnp.bitwise_and(word, 1 << bit) != 0, scale, 0.0
        )

    own_rows = range(REACH, REACH + rows)
    outer_rows = [*range(REACH), *range(REACH + rows, rows + 2 * REACH)]

    for index, (a, b) in enumerate(OFFSETS):
        if in_table(a, b):
            set_masks(index, a, b, 0, rows)
    wait_mid(0)
    place_rows(0, own_rows)
    place_packed(own_rows)
    for index, (a, b) in enumerate(OFFSETS):
        if not in_table(a, b):
            set_masks(index, a, b, -a, rows + a)
    wait_rest(0)
    place_rows(0, outer_rows)
    place_packed(range(REACH))
    for index, (a, b) in enumerate(OFFSETS):
        if a < 0:
            set_masks(index, a, b, 0, -a)

    def forces(phase):
        @pl.loop(0, rows // GROUP)
        def _(group):
            top = group * GROUP
            near = [far[f, REACH, pl.ds(top + REACH, GROUP)] for f in range(4)]
            force_x = jnp.zeros((GROUP, segments, LANES), jnp.float32)
            force_y = jnp.zeros((GROUP, segments, LANES), jnp.float32)
            for index, (a, b) in enumerate(OFFSETS):
                at = pl.ds(top + (REACH + a), GROUP)
                if b == -REACH:
                    near_x = near[0] - float(a)
                rest = STIFFNESS * math.sqrt(a * a + b * b + SOFTENING)
                along_x = far[0, b + REACH, at] - near_x
                along_y = far[1, b + REACH, at] - near[1]
                speed_x = far[2, b + REACH, at] - near[2]
                speed_y = far[3, b + REACH, at] - near[3]
                inverse = lax.rsqrt(along_x * along_x + (along_y * along_y + SOFTENING))
                closing = (along_x * speed_x + along_y * speed_y) * inverse
                if DAMPING != 1.0:
                    closing = closing * DAMPING
                tension = masks[index, pl.ds(top, GROUP)] * (
                    STIFFNESS - inverse * (rest - closing)
                )
                force_x += tension * along_x
                force_y += tension * along_y
            own = pl.ds(top, GROUP)
            for f, force in enumerate((force_x, force_y)):
                kick = (0.5 * TIME_STEP) * force
                value = near[2 + f] + kick
                if 0 < phase < STEPS:
                    value = value + kick
                half[phase, f, own] = value

    for phase in range(STEPS):
        forces(phase)
        for f in range(2):
            for r in range(rows):
                value = half[phase, f, r]
                edges_out[phase, 0, f, r : r + 1, :] = value[0:1]
                edges_out[phase, 1, f, r : r + 1, :] = value[segments - 1 : segments]
        sent.append(copies(phase + 1))
        for c in sent[phase + 1].values():
            c.start()
        wait_mid(phase + 1)
        place_rows(phase + 1, own_rows)
        wait_rest(phase + 1)
        place_rows(phase + 1, outer_rows)
    forces(STEPS)
    for f in range(2):
        disp_out[f] = far[f, REACH, REACH : REACH + rows].reshape(rows, segments * LANES)
        vel_out[f] = half[STEPS, f].reshape(rows, segments * LANES)
    for phase in sent:
        for c in phase.values():
            c.wait_send()


def per_device(disp, vel, bonds):
    rows, columns = disp.shape[1:]
    segments = columns // LANES
    padded = rows + 2 * REACH
    vmem = lambda *shape: pltpu.VMEM(shape, jnp.float32)
    bond_slots = REACH * (REACH + 1) // 2
    spec = pl.BlockSpec(memory_space=pltpu.VMEM)
    return pl.pallas_call(
        kernel,
        out_shape=(jax.ShapeDtypeStruct(disp.shape, disp.dtype),) * 2,
        in_specs=[spec] * 3,
        out_specs=(spec,) * 2,
        scratch_shapes=[
            vmem(4, rows, segments, LANES),
            vmem(4, len(SHIFTS), padded, segments, LANES),
            vmem(STEPS + 1, 2, rows, segments, LANES),
            pltpu.VMEM((len(SHIFTS), REACH + rows, segments, LANES), jnp.int32),
            vmem(len(OFFSETS), rows, segments, LANES),
            vmem(bond_slots, segments, LANES),
            vmem(2, 8, rows, LANES),
            vmem(STEPS, 2, 2, rows, LANES),
            vmem(2, 4, REACH, segments, LANES),
            vmem(bond_slots, segments, LANES),
            vmem(2, 3, 8, rows, LANES),
            vmem(STEPS, 2, 2, REACH, segments, LANES),
            vmem(STEPS, 2, 3, 2, rows, LANES),
            pltpu.SemaphoreType.DMA((STEPS + 1, 9)),
            pltpu.SemaphoreType.DMA((STEPS + 1, 9)),
        ],
        compiler_params=pltpu.CompilerParams(
            collective_id=0, has_side_effects=True, vmem_limit_bytes=32 * 1024 * 1024
        ),
    )(disp, vel, bonds)


def solution(mesh):
    spec = P(None, "gx", "gy")
    return jax.shard_map(
        per_device, mesh=mesh, in_specs=(spec,) * 3, out_specs=(spec,) * 2, check_vma=False
    )
```

time: 60.6 us -> 29.7 us (0.49)
  Pallas kernels: 0 us -> 24.9 us
  starting transfers between devices: 21.7 us -> 0 us
  waiting for transfers between devices: 19.6 us -> 0 us
  other arithmetic: 18.2 us -> 0 us
  local copies, waits for them, and re-layouts: 0.07 us -> 3.84 us
    pallas_call x0 -> x1, Pallas kernels: none -> 24.9 us  [per_device(): pl.pallas_call(kernel, out_shape=(jax.ShapeDtypeStruct(disp.shape, disp.d...]
    ppermute x15 -> x0, starting transfers between devices: 21.7 us -> none  [the longest x7 13.6 us: extended(): lax.ppermute(lax.slice_in_dim(block, 0, width, axis=dim), axis, backward)]
    ppermute x15 -> x0, waiting for transfers between devices: 19.6 us -> none  [the longest x7 10.8 us: extended(): lax.ppermute(lax.slice_in_dim(block, block.shape[dim] - width, None, axis...]
    another operation x6 -> x0, other arithmetic: 15.1 us -> none  [twice_force(): return jnp.stack([force_x, force_y])]
    unnamed x9 -> x8, local copies, waits for them, and re-layouts: 0.03 us -> 3.84 us
    add x5 -> x0, other arithmetic: 1.54 us -> none  [the longest x2 0.86 us: per_device(): packed = bonds[0] + bonds[1] * 8 + bonds[2] * 1024 + bonds[3] * 131072]
    concatenate x11 -> x0, other arithmetic: 1.15 us -> none  [the longest x9 1.11 us: extended(): block = jnp.concatenate([low, block, high], axis=dim)]
  transfers between devices with their start and end apart: 15 -> 0, of which waited for: 11 -> 0; matrix products, arithmetic and copies ran while one was open for 1% -> 0% of each run, Pallas kernels for 0% -> 0%
where the time goes in v1:
time: 29.7 us; the launch traced here: 29.4 us
  Pallas kernels  24.9 us (84%)
  local copies, waits for them, and re-layouts  3.84 us (13%)
  between operations  0.65 us (2%)
    pallas_call x1, Pallas kernels, per_device(): pl.pallas_call(kernel, out_shape=(jax.ShapeDtypeStruct(disp.shape, disp.d...  24.9 us
    unnamed x8, local copies, waits for them, and re-layouts  3.84 us

profile of v1, /device:TPU:1, one launch (start us, length us, event | category | flops | bytes accessed | tf_op | source)
XLA Modules:
  0.0 29.4 jit_solution(3151395177224272312)
XLA Ops:
  0.6 0.0 copy-start
  0.6 0.9 %copy-done = s32[4,8,1024]{2,1,0:T(8,128)S(1)} copy-done((s32[4,8,1024]{2,1,0:T(8,128)S(1)}, s32[4,8,1024]{2,1,0:T(8,128)}, u32[]{:S(2)}) %copy-start) | copy-done | bytes 131096
  1.5 0.0 copy-start.1
  1.5 0.8 %copy-done.1 = f32[2,8,1024]{2,1,0:T(8,128)S(1)} copy-done((f32[2,8,1024]{2,1,0:T(8,128)S(1)}, f32[2,8,1024]{2,1,0:T(8,128)}, u32[]{:S(2)}) %copy-start.1) | copy-done | bytes 65560
  2.4 0.0 copy-start.2
  2.4 0.8 %copy-done.2 = f32[2,8,1024]{2,1,0:T(8,128)S(1)} copy-done((f32[2,8,1024]{2,1,0:T(8,128)S(1)}, f32[2,8,1024]{2,1,0:T(8,128)}, u32[]{:S(2)}) %copy-start.2) | copy-done | bytes 65560
  3.2 24.9 %shard_map.50 = (f32[2,8,1024]{2,1,0:T(8,128)S(1)}, f32[2,8,1024]{2,1,0:T(8,128)S(1)}) custom-call(f32[2,8,1024]{2,1,0:T(8,128)S(1)} %copy-done.1, f32[2,8,1024]{2,1,0:T(8,128)S(1)} %copy-done.2, s32[4,8,1024]{2,1,0:T(8,128)S(1)} %copy-done), custom_call_target="tpu_custom_call" | custom-call | tf_op jit(solution)/shard_map/pallas_call | solution.py:289
  28.1 0.6 %copy.7 = f32[2,8,1024]{2,1,0:T(8,128)} copy(f32[2,8,1024]{2,1,0:T(8,128)S(1)} %get-tuple-element.4) | data formatting | bytes 131072
  28.7 0.6 %copy.8 = f32[2,8,1024]{2,1,0:T(8,128)} copy(f32[2,8,1024]{2,1,0:T(8,128)S(1)} %get-tuple-element.5) | data formatting | bytes 131072
Async XLA Ops:
  0.6 0.9 %copy-start = (s32[4,8,1024]{2,1,0:T(8,128)S(1)}, s32[4,8,1024]{2,1,0:T(8,128)}, u32[]{:S(2)}) copy-start(s32[4,8,1024]{2,1,0:T(8,128)} %bonds_ref.1) | copy-start | bytes 393220
  1.5 0.8 %copy-start.1 = (f32[2,8,1024]{2,1,0:T(8,128)S(1)}, f32[2,8,1024]{2,1,0:T(8,128)}, u32[]{:S(2)}) copy-start(f32[2,8,1024]{2,1,0:T(8,128)} %disp_ref.1) | copy-start | bytes 196612
  2.4 0.8 %copy-start.2 = (f32[2,8,1024]{2,1,0:T(8,128)S(1)}, f32[2,8,1024]{2,1,0:T(8,128)}, u32[]{:S(2)}) copy-start(f32[2,8,1024]{2,1,0:T(8,128)} %vel_ref.1) | copy-start | bytes 196612

commit v2 on v0

v2 whole, which is shorter than its diff:
```python
import functools
import math

import jax
import jax.numpy as jnp
from jax import lax
from jax.experimental import pallas as pl
from jax.experimental.pallas import tpu as pltpu
from jax.sharding import PartitionSpec as P

STEPS = 2
STIFFNESS = 40.0
DAMPING = 1.0
TIME_STEP = 0.05
SOFTENING = 0.0625
REACH = 3
LANES = 128
GROUP = 2
PACK = (1, 8, 1024, 131072)
PACK_SHIFT = (0, 3, 10, 17)
MESH = pl.DeviceIdType.MESH
SHIFTS = tuple(range(-REACH, REACH + 1))


def bond_bit(a, b):
    return b - 1 if a == 0 else PACK_SHIFT[a] + b + REACH


OFFSETS = [(a, b) for a in SHIFTS for b in SHIFTS if (a, b) != (0, 0)]


def in_table(a, b):
    return a > 0 or (a == 0 and b > 0)


def spread(x, low, high, segment, lane):
    segments = x.shape[0]
    after = jnp.where(segment == segments - 1, high, pltpu.roll(x, segments - 1, 0))
    before = jnp.where(segment == 0, low, pltpu.roll(x, 1, 0))
    out = {0: x}
    for b in range(1, REACH + 1):
        out[b] = pltpu.roll(jnp.where(lane < b, after, x), LANES - b, 1)
        out[-b] = pltpu.roll(jnp.where(lane >= LANES - b, before, x), b, 1)
    return out


def kernel(
    disp_ref, vel_ref, bonds_ref, disp_out, vel_out,
    given, given_bonds, state, far, half, packed, masks, total, bond_rows, edge_out, edges_out,
    rows_in, row_bonds_in, edge_in, rows_next, edges_next, load, send, recv,
):
    rows = disp_ref.shape[1]
    segments = disp_ref.shape[2] // LANES
    groups = rows // GROUP
    assert rows % GROUP == 0 and groups >= 4
    loads = [
        pltpu.make_async_copy(disp_ref, given.at[0:2], load.at[0]),
        pltpu.make_async_copy(vel_ref, given.at[2:4], load.at[1]),
        pltpu.make_async_copy(bonds_ref, given_bonds, load.at[2]),
    ]
    for c in loads:
        c.start()

    gx, gy = lax.axis_index("gx"), lax.axis_index("gy")
    nx, ny = lax.axis_size("gx"), lax.axis_size("gy")
    gx_at = {-1: lax.rem(gx + nx - 1, nx), 0: gx, 1: lax.rem(gx + 1, nx)}
    gy_at = {-1: lax.rem(gy + ny - 1, ny), 0: gy, 1: lax.rem(gy + 1, ny)}
    around = [(x, y) for x in (-1, 0, 1) for y in (-1, 0, 1) if (x, y) != (0, 0)]

    barrier = pltpu.get_barrier_semaphore()
    for x, y in around:
        pl.semaphore_signal(
            barrier, inc=1, device_id=(gx_at[x], gy_at[y]), device_id_type=MESH
        )

    def remote(phase, index, src, dst, x, y):
        return pltpu.make_async_remote_copy(
            src_ref=src, dst_ref=dst, send_sem=send.at[phase, index],
            recv_sem=recv.at[phase, index], device_id=(x, y), device_id_type=MESH,
        )

    def row_copy(phase, side):
        start = pl.ds(side * (rows - REACH), REACH)
        x = lax.rem(gx + nx - 1 + 2 * side, nx)
        if phase is None:
            return remote(0, side, state.at[:, start], rows_in.at[1 - side], x, gy)
        return remote(
            phase, side, half.at[phase - 1, :, start], rows_next.at[phase - 1, 1 - side], x, gy
        )

    def bond_copy():
        return remote(0, 2, bond_rows, row_bonds_in, gx_at[1], gy)

    def edge_copy(phase, side, x):
        slot = 1 - x
        index = 3 + 3 * side + slot
        if phase is None:
            planes = 4 if x < 0 else 8
            return remote(
                0, index, edge_out.at[side, 0:planes], edge_in.at[1 - side, slot, 0:planes],
                gx_at[x], gy_at[2 * side - 1],
            )
        return remote(
            phase, index, edges_out.at[phase - 1, side],
            edges_next.at[phase - 1, 1 - side, slot], gx_at[x], gy_at[2 * side - 1],
        )

    def mid_copies(phase):
        return [edge_copy(phase, side, 0) for side in (0, 1)]

    def rest_copies(phase):
        out = [row_copy(phase, side) for side in (0, 1)]
        if phase is None:
            out.append(bond_copy())
        return out + [edge_copy(phase, side, x) for side in (0, 1) for x in (1, -1)]

    def by_segments(block):
        return block.reshape(rows, segments, LANES)

    last = (segments - 1) * LANES
    loads[0].wait()
    loads[1].wait()
    for plane in range(4):
        block = given[plane]
        state[plane] = by_segments(block)
        edge_out[0, plane] = block[:, 0:LANES]
        edge_out[1, plane] = block[:, last : last + LANES]
    loads[2].wait()
    words = []
    for w in range(4):
        word = given_bonds[w].astype(jnp.float32)
        edge_out[0, 4 + w] = word[:, 0:LANES]
        edge_out[1, 4 + w] = word[:, last : last + LANES]
        words.append(by_segments(word))
    slot = 0
    row_bond_slots = {}
    for a in range(1, REACH + 1):
        for r in range(rows - a, rows):
            bond_rows[slot] = words[a][r]
            row_bond_slots[(a, r - rows)] = slot
            slot += 1
    pl.semaphore_wait(barrier, len(around))
    for c in [row_copy(None, 0), row_copy(None, 1)] + mid_copies(None) + rest_copies(None)[2:]:
        c.start()
    own_packed = words[0] * PACK[0] + words[1] * PACK[1] + words[2] * PACK[2] + words[3] * PACK[3]
    packed[...] = own_packed.astype(jnp.int32)

    segment = lax.broadcasted_iota(jnp.int32, (segments, LANES), 0)
    lane = lax.broadcasted_iota(jnp.int32, (segments, LANES), 1)

    def mask_index(a, b):
        return (a + REACH) * len(SHIFTS) + b + REACH

    def mask(word, bit, a, b):
        return jnp.where(jnp.bitwise_and(word, 1 << bit) != 0, 1.0 / (a * a + b * b), 0.0)

    def push_masks(r, word, low, high):
        for b, value in spread(word, low, high, segment, lane).items():
            for a in range(REACH + 1):
                if in_table(a, -b):
                    masks[mask_index(-a, b), r + REACH + a] = mask(value, bond_bit(a, -b), a, b)

    def edge_word(slot, e):
        out = []
        for side in (0, 1):
            value = edge_in[side, slot, 4, pl.ds(e, 1), :]
            for w in range(1, 4):
                value = value + edge_in[side, slot, 4 + w, pl.ds(e, 1), :] * PACK[w]
            out.append(value.astype(jnp.int32))
        return out

    def place_first(r, rows_of, slot, e):
        for plane in range(4):
            low = edge_in[0, slot, plane, pl.ds(e, 1), :]
            high = edge_in[1, slot, plane, pl.ds(e, 1), :]
            for b, value in spread(rows_of(plane), low, high, segment, lane).items():
                far[plane, b + REACH, r + REACH] = value + float(b) if plane == 1 and b else value

    def place_next(phase, r, rows_of, slot, e):
        for plane in range(2):
            low = edges_next[phase - 1, 0, slot, plane, pl.ds(e, 1), :]
            high = edges_next[phase - 1, 1, slot, plane, pl.ds(e, 1), :]
            for b, value in spread(rows_of(plane), low, high, segment, lane).items():
                far[2 + plane, b + REACH, r + REACH] = value
                far[plane, b + REACH, r + REACH] += TIME_STEP * value

    @pl.loop(0, rows)
    def _(r):
        word = packed[r]
        for a, b in OFFSETS:
            if in_table(a, b):
                masks[mask_index(a, b), r + REACH] = mask(word, bond_bit(a, b), a, b)

    def evaluate(near, top, signed, sums):
        force_x, force_y = sums
        for a, size in signed:
            near_x = near[0] - lax.convert_element_type(a, jnp.float32)
            at = pl.ds(top + REACH + a, GROUP)
            for b in SHIFTS:
                if size == 0 and b == 0:
                    continue
                rest = STIFFNESS * math.sqrt(size * size + b * b + SOFTENING)
                along_x = far[0, b + REACH, at] - near_x
                along_y = far[1, b + REACH, at] - near[1]
                speed_x = far[2, b + REACH, at] - near[2]
                speed_y = far[3, b + REACH, at] - near[3]
                inverse = lax.rsqrt(along_x * along_x + (along_y * along_y + SOFTENING))
                closing = (along_x * speed_x + along_y * speed_y) * inverse
                if DAMPING != 1.0:
                    closing = closing * DAMPING
                tension = masks[mask_index(a, b), pl.ds(top + REACH, GROUP)] * (
                    STIFFNESS - inverse * (rest - closing)
                )
                force_x += tension * along_x
                force_y += tension * along_y
        return force_x, force_y

    def near_of(top):
        return [far[f, REACH, pl.ds(top + REACH, GROUP)] for f in range(4)]

    zero = jnp.zeros((GROUP, segments, LANES), jnp.float32)

    def inner_forces():
        @pl.loop(0, 2)
        def _(side):
            sign = 1 - 2 * side
            for depth, sizes in ((0, range(0, REACH + 1)), (1, range(-2, REACH + 1))):
                top = depth * GROUP + side * (rows - (2 * depth + 1) * GROUP)
                signed = [(sign * a, abs(a)) for a in sizes]
                sums = evaluate(near_of(top), top, signed, (zero, zero))
                for f in range(2):
                    total[f, pl.ds(top, GROUP)] = sums[f]

        if groups > 4:
            @pl.loop(2, groups - 2)
            def _(group):
                top = group * GROUP
                sums = evaluate(near_of(top), top, [(a, abs(a)) for a in SHIFTS], (zero, zero))
                for f in range(2):
                    total[f, pl.ds(top, GROUP)] = sums[f]

    def kicked(phase, top, near, sums):
        again = jnp.where(jnp.logical_and(phase > 0, phase < STEPS), 1.0, 0.0)
        for f in range(2):
            kick = (0.5 * TIME_STEP) * sums[f]
            value = (near[2 + f] + kick) + kick * again
            half[phase, f, pl.ds(top, GROUP)] = value
            for k in range(GROUP):
                edges_out[phase, 0, f, pl.ds(top + k, 1), :] = value[k, 0:1]
                edges_out[phase, 1, f, pl.ds(top + k, 1), :] = value[k, segments - 1 : segments]

    def outer_forces(phase):
        if groups > 4:
            @pl.loop(2, groups - 2)
            def _(group):
                top = group * GROUP
                kicked(phase, top, near_of(top), [total[f, pl.ds(top, GROUP)] for f in range(2)])

        @pl.loop(0, 2)
        def _(side):
            sign = 1 - 2 * side
            for depth, sizes in ((0, (-1, -2, -3)), (1, (-3,))):
                top = depth * GROUP + side * (rows - (2 * depth + 1) * GROUP)
                near = near_of(top)
                sums = [total[f, pl.ds(top, GROUP)] for f in range(2)]
                signed = [(sign * a, abs(a)) for a in sizes]
                kicked(phase, top, near, evaluate(near, top, signed, sums))

            @pl.when(phase < STEPS)
            def _():
                row_copy(phase + 1, side).start()

    @pl.loop(0, STEPS + 1)
    def _(phase):
        @pl.when(phase == 0)
        def _():
            for c in mid_copies(None):
                c.wait_recv()

            @pl.loop(0, rows)
            def _(r):
                place_first(r, lambda plane: state[plane, r], 1, r)
                push_masks(r, packed[r], *edge_word(1, r))

        @pl.when(phase > 0)
        def _():
            for c in mid_copies(phase):
                c.wait_recv()

            @pl.loop(0, groups)
            def _(group):
                for k in range(GROUP):
                    r = group * GROUP + k
                    place_next(phase, r, lambda plane: half[phase - 1, plane, r], 1, r)

        inner_forces()

        @pl.when(phase == 0)
        def _():
            for c in rest_copies(None):
                c.wait_recv()

            @pl.loop(0, REACH)
            def _(k):
                r = k - REACH
                place_first(r, lambda plane: rows_in[0, plane, k], 0, rows - REACH + k)
                place_first(rows + k, lambda plane: rows_in[1, plane, k], 2, k)

            for r in range(-REACH, 0):
                word = jnp.zeros((segments, LANES), jnp.float32)
                for a in range(-r, REACH + 1):
                    word = word + row_bonds_in[row_bond_slots[(a, r)]] * PACK[a]
                push_masks(r, word.astype(jnp.int32), *edge_word(0, rows + r))

        @pl.when(phase > 0)
        def _():
            for c in rest_copies(phase):
                c.wait_recv()

            @pl.loop(0, REACH)
            def _(k):
                place_next(
                    phase, k - REACH, lambda plane: rows_next[phase - 1, 0, plane, k], 0,
                    rows - REACH + k,
                )
                place_next(
                    phase, rows + k, lambda plane: rows_next[phase - 1, 1, plane, k], 2, k
                )

        outer_forces(phase)

        @pl.when(phase < STEPS)
        def _():
            for c in mid_copies(phase + 1) + rest_copies(phase + 1)[2:]:
                c.start()

    for f in range(2):
        disp_out[f] = far[f, REACH, REACH : REACH + rows].reshape(rows, segments * LANES)
        vel_out[f] = half[STEPS, f].reshape(rows, segments * LANES)
    for phase in [None, *range(1, STEPS + 1)]:
        for c in mid_copies(phase) + rest_copies(phase):
            c.wait_send()


def per_device(disp, vel, bonds):
    rows, columns = disp.shape[1:]
    segments = columns // LANES
    padded = rows + 2 * REACH
    vmem = lambda *shape: pltpu.VMEM(shape, jnp.float32)
    bond_slots = REACH * (REACH + 1) // 2
    spec = pl.BlockSpec(memory_space=pltpu.VMEM)
    return pl.pallas_call(
        kernel,
        out_shape=(jax.ShapeDtypeStruct(disp.shape, disp.dtype),) * 2,
        in_specs=[pl.BlockSpec(memory_space=pl.ANY)] * 3,
        out_specs=(spec,) * 2,
        scratch_shapes=[
            vmem(4, rows, columns),
            pltpu.VMEM((4, rows, columns), jnp.int32),
            vmem(4, rows, segments, LANES),
            vmem(4, len(SHIFTS), padded, segments, LANES),
            vmem(STEPS + 1, 2, rows, segments, LANES),
            pltpu.VMEM((rows, segments, LANES), jnp.int32),
            vmem(len(SHIFTS) ** 2, padded, segments, LANES),
            vmem(2, rows, segments, LANES),
            vmem(bond_slots, segments, LANES),
            vmem(2, 8, rows, LANES),
            vmem(STEPS + 1, 2, 2, rows, LANES),
            vmem(2, 4, REACH, segments, LANES),
            vmem(bond_slots, segments, LANES),
            vmem(2, 3, 8, rows, LANES),
            vmem(STEPS, 2, 2, REACH, segments, LANES),
            vmem(STEPS, 2, 3, 2, rows, LANES),
            pltpu.SemaphoreType.DMA((3,)),
            pltpu.SemaphoreType.DMA((STEPS + 1, 9)),
            pltpu.SemaphoreType.DMA((STEPS + 1, 9)),
        ],
        compiler_params=pltpu.CompilerParams(
            collective_id=0, has_side_effects=True, vmem_limit_bytes=56 * 1024 * 1024
        ),
    )(disp, vel, bonds)


def solution(mesh):
    spec = P(None, "gx", "gy")
    return jax.shard_map(
        per_device, mesh=mesh, in_specs=(spec,) * 3, out_specs=(spec,) * 2, check_vma=False
    )
```

time: 60.6 us -> 26.9 us (0.44)
  Pallas kernels: 0 us -> 23.9 us
  starting transfers between devices: 21.7 us -> 0 us
  waiting for transfers between devices: 19.6 us -> 0 us
  other arithmetic: 18.2 us -> 0 us
  local copies, waits for them, and re-layouts: 0.07 us -> 2.14 us
    pallas_call x0 -> x1, Pallas kernels: none -> 23.9 us  [per_device(): pl.pallas_call(kernel, out_shape=(jax.ShapeDtypeStruct(disp.shape, disp.d...]
    ppermute x15 -> x0, starting transfers between devices: 21.7 us -> none  [the longest x7 13.6 us: extended(): lax.ppermute(lax.slice_in_dim(block, 0, width, axis=dim), axis, backward)]
    ppermute x15 -> x0, waiting for transfers between devices: 19.6 us -> none  [the longest x7 10.8 us: extended(): lax.ppermute(lax.slice_in_dim(block, block.shape[dim] - width, None, axis...]
    another operation x6 -> x0, other arithmetic: 15.1 us -> none  [twice_force(): return jnp.stack([force_x, force_y])]
    unnamed x9 -> x4, local copies, waits for them, and re-layouts: 0.03 us -> 2.14 us
    add x5 -> x0, other arithmetic: 1.54 us -> none  [the longest x2 0.86 us: per_device(): packed = bonds[0] + bonds[1] * 8 + bonds[2] * 1024 + bonds[3] * 131072]
    concatenate x11 -> x0, other arithmetic: 1.15 us -> none  [the longest x9 1.11 us: extended(): block = jnp.concatenate([low, block, high], axis=dim)]
  transfers between devices with their start and end apart: 15 -> 0, of which waited for: 11 -> 0; matrix products, arithmetic and copies ran while one was open for 1% -> 0% of each run, Pallas kernels for 0% -> 0%
where the time goes in v2:
time: 26.9 us; the launch traced here: 26.7 us
  Pallas kernels  23.9 us (89%)
  local copies, waits for them, and re-layouts  2.14 us (8%)
  between operations  0.65 us (2%)
    pallas_call x1, Pallas kernels, per_device(): pl.pallas_call(kernel, out_shape=(jax.ShapeDtypeStruct(disp.shape, disp.d...  23.9 us
    unnamed x4, local copies, waits for them, and re-layouts  2.14 us

profile of v2, /device:TPU:1, one launch (start us, length us, event | category | flops | bytes accessed | tf_op | source)
XLA Modules:
  0.0 26.7 jit_solution(4278989648926838324)
XLA Ops:
  0.6 23.9 %shard_map.50 = (f32[2,8,1024]{2,1,0:T(8,128)}, f32[2,8,1024]{2,1,0:T(8,128)}) custom-call(f32[2,8,1024]{2,1,0:T(8,128)} %disp_ref.1, f32[2,8,1024]{2,1,0:T(8,128)} %vel_ref.1, s32[4,8,1024]{2,1,0:T(8,128)} %bonds_ref.1), custom_call_target="tpu_custom_call" | custom-call | tf_op jit(solution)/shard_map/pallas_call | solution.py:352
  24.6 0.0 copy-start
  24.6 1.5 %copy.7 = f32[2,8,1024]{2,1,0:T(8,128)} copy(f32[2,8,1024]{2,1,0:T(8,128)} %get-tuple-element.4) | data formatting | bytes 131072
  26.1 0.0 copy-done
  26.1 0.6 %copy.8 = f32[2,8,1024]{2,1,0:T(8,128)} copy(f32[2,8,1024]{2,1,0:T(8,128)S(1)} %copy-done) | data formatting | bytes 131072
Async XLA Ops:
  24.6 1.5 %copy-start = (f32[2,8,1024]{2,1,0:T(8,128)S(1)}, f32[2,8,1024]{2,1,0:T(8,128)}, u32[]{:S(2)}) copy-start(f32[2,8,1024]{2,1,0:T(8,128)} %get-tuple-element.5) | copy-start | bytes 196612

commit v3 on v2

--- a/solution.py
+++ b/solution.py
@@ -47,12 +47,15 @@
 def kernel(
     disp_ref, vel_ref, bonds_ref, disp_out, vel_out,
     given, given_bonds, state, far, half, packed, masks, total, bond_rows, edge_out, edges_out,
-    rows_in, row_bonds_in, edge_in, rows_next, edges_next, load, send, recv,
+    corner_out, corners_out, rows_in, row_bonds_in, edge_in, corner_in, rows_next, edges_next,
+    corners_next, load, send, recv,
 ):
     rows = disp_ref.shape[1]
     segments = disp_ref.shape[2] // LANES
     groups = rows // GROUP
     assert rows % GROUP == 0 and groups >= 4
+    corner_rows = corner_out.shape[2]
+    corner_state = 16
     loads = [
         pltpu.make_async_copy(disp_ref, given.at[0:2], load.at[0]),
         pltpu.make_async_copy(vel_ref, given.at[2:4], load.at[1]),
@@ -91,28 +94,40 @@
     def bond_copy():
         return remote(0, 2, bond_rows, row_bonds_in, gx_at[1], gy)
 
-    def edge_copy(phase, side, x):
-        slot = 1 - x
-        index = 3 + 3 * side + slot
+    def edge_copy(phase, side):
+        y = gy_at[2 * side - 1]
         if phase is None:
-            planes = 4 if x < 0 else 8
+            return remote(0, 3 + side, edge_out.at[side], edge_in.at[1 - side], gx, y)
+        return remote(
+            phase, 3 + side, edges_out.at[phase - 1, side], edges_next.at[phase - 1, 1 - side], gx, y
+        )
+
+    def corner_copy(phase, along, across, first_rows=0):
+        x = lax.rem(gx + nx - 1 + 2 * along, nx)
+        y = gy_at[2 * across - 1]
+        index = 5 + 2 * along + across
+        if phase is None:
+            part = pl.ds(0, first_rows)
             return remote(
-                0, index, edge_out.at[side, 0:planes], edge_in.at[1 - side, slot, 0:planes],
-                gx_at[x], gy_at[2 * side - 1],
+                0, index, corner_out.at[along, across, part],
+                corner_in.at[1 - along, 1 - across, part], x, y,
             )
         return remote(
-            phase, index, edges_out.at[phase - 1, side],
-            edges_next.at[phase - 1, 1 - side, slot], gx_at[x], gy_at[2 * side - 1],
+            phase, index, corners_out.at[phase - 1, along, across],
+            corners_next.at[phase - 1, 1 - along, 1 - across], x, y,
         )
 
     def mid_copies(phase):
-        return [edge_copy(phase, side, 0) for side in (0, 1)]
+        return [edge_copy(phase, side) for side in (0, 1)]
 
     def rest_copies(phase):
         out = [row_copy(phase, side) for side in (0, 1)]
         if phase is None:
             out.append(bond_copy())
-        return out + [edge_copy(phase, side, x) for side in (0, 1) for x in (1, -1)]
+        return out + [
+            corner_copy(phase, along, across, (corner_state, corner_rows)[along])
+            for along in (0, 1) for across in (0, 1)
+        ]
 
     def by_segments(block):
         return block.reshape(rows, segments, LANES)
@@ -125,6 +140,11 @@
         state[plane] = by_segments(block)
         edge_out[0, plane] = block[:, 0:LANES]
         edge_out[1, plane] = block[:, last : last + LANES]
+        for along in (0, 1):
+            top = along * (rows - REACH)
+            at = slice(plane * REACH, (plane + 1) * REACH)
+            corner_out[along, 0, at] = block[top : top + REACH, 0:LANES]
+            corner_out[along, 1, at] = block[top : top + REACH, last : last + LANES]
     loads[2].wait()
     words = []
     for w in range(4):
@@ -137,10 +157,13 @@
     for a in range(1, REACH + 1):
         for r in range(rows - a, rows):
             bond_rows[slot] = words[a][r]
+            for across in (0, 1):
+                at = corner_state + slot
+                corner_out[1, across, at : at + 1] = edge_out[across, 4 + a, r : r + 1]
             row_bond_slots[(a, r - rows)] = slot
             slot += 1
     pl.semaphore_wait(barrier, len(around))
-    for c in [row_copy(None, 0), row_copy(None, 1)] + mid_copies(None) + rest_copies(None)[2:]:
+    for c in rest_copies(None) + mid_copies(None):
         c.start()
     own_packed = words[0] * PACK[0] + words[1] * PACK[1] + words[2] * PACK[2] + words[3] * PACK[3]
     packed[...] = own_packed.astype(jnp.int32)
@@ -160,26 +183,15 @@
                 if in_table(a, -b):
                     masks[mask_index(-a, b), r + REACH + a] = mask(value, bond_bit(a, -b), a, b)
 
-    def edge_word(slot, e):
-        out = []
-        for side in (0, 1):
-            value = edge_in[side, slot, 4, pl.ds(e, 1), :]
-            for w in range(1, 4):
-                value = value + edge_in[side, slot, 4 + w, pl.ds(e, 1), :] * PACK[w]
-            out.append(value.astype(jnp.int32))
-        return out
-
-    def place_first(r, rows_of, slot, e):
+    def place_first(r, rows_of, outer):
         for plane in range(4):
-            low = edge_in[0, slot, plane, pl.ds(e, 1), :]
-            high = edge_in[1, slot, plane, pl.ds(e, 1), :]
+            low, high = outer(0, plane), outer(1, plane)
             for b, value in spread(rows_of(plane), low, high, segment, lane).items():
                 far[plane, b + REACH, r + REACH] = value + float(b) if plane == 1 and b else value
 
-    def place_next(phase, r, rows_of, slot, e):
+    def place_next(r, rows_of, outer):
         for plane in range(2):
-            low = edges_next[phase - 1, 0, slot, plane, pl.ds(e, 1), :]
-            high = edges_next[phase - 1, 1, slot, plane, pl.ds(e, 1), :]
+            low, high = outer(0, plane), outer(1, plane)
             for b, value in spread(rows_of(plane), low, high, segment, lane).items():
                 far[2 + plane, b + REACH, r + REACH] = value
                 far[plane, b + REACH, r + REACH] += TIME_STEP * value
@@ -269,6 +281,15 @@
             @pl.when(phase < STEPS)
             def _():
                 row_copy(phase + 1, side).start()
+                for f in range(2):
+                    for k in range(REACH):
+                        r = side * (rows - REACH) + k
+                        for across in (0, 1):
+                            corners_out[phase, side, across, f * REACH + k : f * REACH + k + 1, :] = (
+                                edges_out[phase, across, f, pl.ds(r, 1), :]
+                            )
+                for across in (0, 1):
+                    corner_copy(phase + 1, side, across).start()
 
     @pl.loop(0, STEPS + 1)
     def _(phase):
@@ -277,21 +298,35 @@
             for c in mid_copies(None):
                 c.wait_recv()
 
-            @pl.loop(0, rows)
-            def _(r):
-                place_first(r, lambda plane: state[plane, r], 1, r)
-                push_masks(r, packed[r], *edge_word(1, r))
+            @pl.loop(0, groups)
+            def _(group):
+                for k in range(GROUP):
+                    r = group * GROUP + k
+                    place_first(
+                        r, lambda plane: state[plane, r],
+                        lambda side, plane: edge_in[side, plane, pl.ds(r, 1), :],
+                    )
+                    outer = []
+                    for side in (0, 1):
+                        value = edge_in[side, 4, pl.ds(r, 1), :]
+                        for w in range(1, 4):
+                            value = value + edge_in[side, 4 + w, pl.ds(r, 1), :] * PACK[w]
+                        outer.append(value.astype(jnp.int32))
+                    push_masks(r, packed[r], *outer)
 
         @pl.when(phase > 0)
         def _():
             for c in mid_copies(phase):
                 c.wait_recv()
 
-            @pl.loop(0, groups)
+            @pl.loop(0, groups // 2)
             def _(group):
-                for k in range(GROUP):
-                    r = group * GROUP + k
-                    place_next(phase, r, lambda plane: half[phase - 1, plane, r], 1, r)
+                for k in range(2 * GROUP):
+                    r = group * (2 * GROUP) + k
+                    place_next(
+                        r, lambda plane: half[phase - 1, plane, r],
+                        lambda side, plane: edges_next[phase - 1, side, plane, pl.ds(r, 1), :],
+                    )
 
         inner_forces()
 
@@ -300,38 +335,46 @@
             for c in rest_copies(None):
                 c.wait_recv()
 
-            @pl.loop(0, REACH)
-            def _(k):
-                r = k - REACH
-                place_first(r, lambda plane: rows_in[0, plane, k], 0, rows - REACH + k)
-                place_first(rows + k, lambda plane: rows_in[1, plane, k], 2, k)
+            for along in (0, 1):
+                for k in range(REACH):
+                    place_first(
+                        along * (rows + REACH) - REACH + k, lambda plane: rows_in[along, plane, k],
+                        lambda side, plane: corner_in[
+                            along, side, plane * REACH + k : plane * REACH + k + 1, :
+                        ],
+                    )
 
             for r in range(-REACH, 0):
                 word = jnp.zeros((segments, LANES), jnp.float32)
+                outer = [jnp.zeros((1, LANES), jnp.float32) for side in (0, 1)]
                 for a in range(-r, REACH + 1):
-                    word = word + row_bonds_in[row_bond_slots[(a, r)]] * PACK[a]
-                push_masks(r, word.astype(jnp.int32), *edge_word(0, rows + r))
+                    slot = row_bond_slots[(a, r)]
+                    at = corner_state + slot
+                    word = word + row_bonds_in[slot] * PACK[a]
+                    for side in (0, 1):
+                        outer[side] += corner_in[0, side, at : at + 1, :] * PACK[a]
+                push_masks(r, word.astype(jnp.int32), *[x.astype(jnp.int32) for x in outer])
 
         @pl.when(phase > 0)
         def _():
             for c in rest_copies(phase):
                 c.wait_recv()
 
-            @pl.loop(0, REACH)
-            def _(k):
-                place_next(
-                    phase, k - REACH, lambda plane: rows_next[phase - 1, 0, plane, k], 0,
-                    rows - REACH + k,
-                )
-                place_next(
-                    phase, rows + k, lambda plane: rows_next[phase - 1, 1, plane, k], 2, k
-                )
+            for along in (0, 1):
+                for k in range(REACH):
+                    place_next(
+                        along * (rows + REACH) - REACH + k,
+                        lambda plane: rows_next[phase - 1, along, plane, k],
+                        lambda side, plane: corners_next[
+                            phase - 1, along, side, plane * REACH + k : plane * REACH + k + 1, :
+                        ],
+                    )
 
         outer_forces(phase)
 
         @pl.when(phase < STEPS)
         def _():
-            for c in mid_copies(phase + 1) + rest_copies(phase + 1)[2:]:
+            for c in mid_copies(phase + 1):
                 c.start()
 
     for f in range(2):
@@ -340,6 +383,17 @@
     for phase in [None, *range(1, STEPS + 1)]:
         for c in mid_copies(phase) + rest_copies(phase):
             c.wait_send()
+
+
+def store(disp_ref, vel_ref, disp_out, vel_out, sems):
+    copies = [
+        pltpu.make_async_copy(disp_ref, disp_out, sems.at[0]),
+        pltpu.make_async_copy(vel_ref, vel_out, sems.at[1]),
+    ]
+    for c in copies:
+        c.start()
+    for c in copies:
+        c.wait()
 
 
 def per_device(disp, vel, bonds):
@@ -349,10 +403,11 @@
     vmem = lambda *shape: pltpu.VMEM(shape, jnp.float32)
     bond_slots = REACH * (REACH + 1) // 2
     spec = pl.BlockSpec(memory_space=pltpu.VMEM)
-    return pl.pallas_call(
+    results = (jax.ShapeDtypeStruct(disp.shape, disp.dtype),) * 2
+    done = pl.pallas_call(
         kernel,
-        out_shape=(jax.ShapeDtypeStruct(disp.shape, disp.dtype),) * 2,
-        in_specs=[pl.BlockSpec(memory_space=pl.ANY)] * 3,
+        out_shape=results,
+        in_specs=[pl.BlockSpec(memory_space=pltpu.HBM)] * 3,
         out_specs=(spec,) * 2,
         scratch_shapes=[
             vmem(4, rows, columns),
@@ -366,19 +421,30 @@
             vmem(bond_slots, segments, LANES),
             vmem(2, 8, rows, LANES),
             vmem(STEPS + 1, 2, 2, rows, LANES),
+            vmem(2, 2, 24, LANES),
+            vmem(STEPS, 2, 2, 8, LANES),
             vmem(2, 4, REACH, segments, LANES),
             vmem(bond_slots, segments, LANES),
-            vmem(2, 3, 8, rows, LANES),
+            vmem(2, 8, rows, LANES),
+            vmem(2, 2, 24, LANES),
             vmem(STEPS, 2, 2, REACH, segments, LANES),
-            vmem(STEPS, 2, 3, 2, rows, LANES),
+            vmem(STEPS, 2, 2, rows, LANES),
+            vmem(STEPS, 2, 2, 8, LANES),
             pltpu.SemaphoreType.DMA((3,)),
             pltpu.SemaphoreType.DMA((STEPS + 1, 9)),
             pltpu.SemaphoreType.DMA((STEPS + 1, 9)),
         ],
         compiler_params=pltpu.CompilerParams(
-            collective_id=0, has_side_effects=True, vmem_limit_bytes=56 * 1024 * 1024
+            collective_id=0, has_side_effects=True, vmem_limit_bytes=20 * 1024 * 1024
         ),
     )(disp, vel, bonds)
+    return pl.pallas_call(
+        store,
+        out_shape=results,
+        in_specs=[spec] * 2,
+        out_specs=(pl.BlockSpec(memory_space=pltpu.HBM),) * 2,
+        scratch_shapes=[pltpu.SemaphoreType.DMA((2,))],
+    )(*done)
 
 
 def solution(mesh):

time: 26.9 us -> 28.6 us (1.063)
  local copies, waits for them, and re-layouts: 2.14 us -> 3.8 us
    unnamed x4 -> x10, local copies, waits for them, and re-layouts: 2.14 us -> 3.8 us
    pallas_call x1 -> x2, Pallas kernels: 23.9 us -> 23.9 us  [the longest x1 22.3 us: per_device(): pl.pallas_call(kernel, out_shape=results, in_specs=[pl.BlockSpec(memory_s...]
where the time goes in v3:
time: 28.6 us; the launch traced here: 28.3 us
  Pallas kernels  23.9 us (84%)
  local copies, waits for them, and re-layouts  3.8 us (13%)
  between operations  0.66 us (2%)
    pallas_call x1, Pallas kernels, per_device(): pl.pallas_call(kernel, out_shape=results, in_specs=[pl.BlockSpec(memory_s...  22.3 us
    unnamed x10, local copies, waits for them, and re-layouts  3.8 us
    pallas_call x1, Pallas kernels, per_device(): pl.pallas_call(store, out_shape=results, in_specs=[spec] * 2, out_specs=(...  1.54 us

profile of v3, /device:TPU:1, one launch (start us, length us, event | category | flops | bytes accessed | tf_op | source)
XLA Modules:
  0.0 28.3 jit_solution(2103389238673439857)
XLA Ops:
  0.6 0.0 copy-start
  0.6 0.9 %copy-done = s32[4,8,1024]{2,1,0:T(8,128)S(1)} copy-done((s32[4,8,1024]{2,1,0:T(8,128)S(1)}, s32[4,8,1024]{2,1,0:T(8,128)}, u32[]{:S(2)}) %copy-start) | copy-done | bytes 131096
  1.5 0.0 copy-start.3
  1.5 0.8 %copy-done.3 = f32[2,8,1024]{2,1,0:T(8,128)S(1)} copy-done((f32[2,8,1024]{2,1,0:T(8,128)S(1)}, f32[2,8,1024]{2,1,0:T(8,128)}, u32[]{:S(2)}) %copy-start.3) | copy-done | bytes 65560
  2.4 0.0 copy-start.4
  2.4 0.8 %copy-done.4 = f32[2,8,1024]{2,1,0:T(8,128)S(1)} copy-done((f32[2,8,1024]{2,1,0:T(8,128)S(1)}, f32[2,8,1024]{2,1,0:T(8,128)}, u32[]{:S(2)}) %copy-start.4) | copy-done | bytes 65560
  3.2 22.3 %shard_map.50 = (f32[2,8,1024]{2,1,0:T(8,128)S(1)}, f32[2,8,1024]{2,1,0:T(8,128)S(1)}) custom-call(f32[2,8,1024]{2,1,0:T(8,128)S(1)} %copy-done.3, f32[2,8,1024]{2,1,0:T(8,128)S(1)} %copy-done.4, s32[4,8,1024]{2,1,0:T(8,128)S(1)} %copy-done), custom_call_target="tpu_custom_call" | custom-call | tf_op jit(solution)/shard_map/pallas_call | solution.py:407
  25.6 0.0 copy-start.1
  25.6 0.6 %copy-done.1 = f32[2,8,1024]{2,1,0:T(8,128)} copy-done((f32[2,8,1024]{2,1,0:T(8,128)}, f32[2,8,1024]{2,1,0:T(8,128)S(1)}, u32[]{:S(2)}) %copy-start.1) | copy-done | bytes 65560
  26.2 0.0 copy-start.2
  26.2 0.6 %copy-done.2 = f32[2,8,1024]{2,1,0:T(8,128)} copy-done((f32[2,8,1024]{2,1,0:T(8,128)}, f32[2,8,1024]{2,1,0:T(8,128)S(1)}, u32[]{:S(2)}) %copy-start.2) | copy-done | bytes 65560
  26.8 1.5 %shard_map.51 = (f32[2,8,1024]{2,1,0:T(8,128)}, f32[2,8,1024]{2,1,0:T(8,128)}) custom-call(f32[2,8,1024]{2,1,0:T(8,128)} %copy-done.1, f32[2,8,1024]{2,1,0:T(8,128)} %copy-done.2), custom_call_target="tpu_custom_call" | custom-call | tf_op jit(solution)/shard_map/pallas_call | solution.py:441
Async XLA Ops:
  0.6 0.9 %copy-start = (s32[4,8,1024]{2,1,0:T(8,128)S(1)}, s32[4,8,1024]{2,1,0:T(8,128)}, u32[]{:S(2)}) copy-start(s32[4,8,1024]{2,1,0:T(8,128)} %bonds_ref.1) | copy-start | bytes 393220
  1.5 0.8 %copy-start.3 = (f32[2,8,1024]{2,1,0:T(8,128)S(1)}, f32[2,8,1024]{2,1,0:T(8,128)}, u32[]{:S(2)}) copy-start(f32[2,8,1024]{2,1,0:T(8,128)} %disp_ref.1) | copy-start | bytes 196612
  2.4 0.8 %copy-start.4 = (f32[2,8,1024]{2,1,0:T(8,128)S(1)}, f32[2,8,1024]{2,1,0:T(8,128)}, u32[]{:S(2)}) copy-start(f32[2,8,1024]{2,1,0:T(8,128)} %vel_ref.1) | copy-start | bytes 196612
  25.6 0.6 %copy-start.1 = (f32[2,8,1024]{2,1,0:T(8,128)}, f32[2,8,1024]{2,1,0:T(8,128)S(1)}, u32[]{:S(2)}) copy-start(f32[2,8,1024]{2,1,0:T(8,128)S(1)} %get-tuple-element.4.disp_ref) | copy-start | bytes 196612
  26.2 0.6 %copy-start.2 = (f32[2,8,1024]{2,1,0:T(8,128)}, f32[2,8,1024]{2,1,0:T(8,128)S(1)}, u32[]{:S(2)}) copy-start(f32[2,8,1024]{2,1,0:T(8,128)S(1)} %get-tuple-element.5.vel_ref) | copy-start | bytes 196612

commit v4 on v3

--- a/solution.py
+++ b/solution.py
@@ -385,17 +385,6 @@
             c.wait_send()
 
 
-def store(disp_ref, vel_ref, disp_out, vel_out, sems):
-    copies = [
-        pltpu.make_async_copy(disp_ref, disp_out, sems.at[0]),
-        pltpu.make_async_copy(vel_ref, vel_out, sems.at[1]),
-    ]
-    for c in copies:
-        c.start()
-    for c in copies:
-        c.wait()
-
-
 def per_device(disp, vel, bonds):
     rows, columns = disp.shape[1:]
     segments = columns // LANES
@@ -404,7 +393,7 @@
     bond_slots = REACH * (REACH + 1) // 2
     spec = pl.BlockSpec(memory_space=pltpu.VMEM)
     results = (jax.ShapeDtypeStruct(disp.shape, disp.dtype),) * 2
-    done = pl.pallas_call(
+    return pl.pallas_call(
         kernel,
         out_shape=results,
         in_specs=[pl.BlockSpec(memory_space=pltpu.HBM)] * 3,
@@ -435,16 +424,9 @@
             pltpu.SemaphoreType.DMA((STEPS + 1, 9)),
         ],
         compiler_params=pltpu.CompilerParams(
-            collective_id=0, has_side_effects=True, vmem_limit_bytes=20 * 1024 * 1024
+            collective_id=0, has_side_effects=True, vmem_limit_bytes=55104 * 1024
         ),
     )(disp, vel, bonds)
-    return pl.pallas_call(
-        store,
-        out_shape=results,
-        in_specs=[spec] * 2,
-        out_specs=(pl.BlockSpec(memory_space=pltpu.HBM),) * 2,
-        scratch_shapes=[pltpu.SemaphoreType.DMA((2,))],
-    )(*done)
 
 
 def solution(mesh):

time: 28.6 us -> 24.1 us (0.84)
  local copies, waits for them, and re-layouts: 3.8 us -> 1.26 us
  Pallas kernels: 23.9 us -> 22.1 us
    unnamed x10 -> x2, local copies, waits for them, and re-layouts: 3.8 us -> 1.26 us
    pallas_call x1 -> x0, Pallas kernels: 1.54 us -> none  [per_device(): pl.pallas_call(store, out_shape=results, in_specs=[spec] * 2, out_specs=(...]
where the time goes in v4:
time: 24.1 us; the launch traced here: 23.9 us
  Pallas kernels  22.1 us (92%)
  local copies, waits for them, and re-layouts  1.26 us (5%)
  between operations  0.64 us (3%)
    pallas_call x1, Pallas kernels, per_device(): pl.pallas_call(kernel, out_shape=results, in_specs=[pl.BlockSpec(memory_s...  22.1 us
    unnamed x2, local copies, waits for them, and re-layouts  1.26 us

profile of v4, /device:TPU:1, one launch (start us, length us, event | category | flops | bytes accessed | tf_op | source)
XLA Modules:
  0.0 23.9 jit_solution(3237936361073982722)
XLA Ops:
  0.6 22.1 %shard_map.50 = (f32[2,8,1024]{2,1,0:T(8,128)S(1)}, f32[2,8,1024]{2,1,0:T(8,128)S(1)}) custom-call(f32[2,8,1024]{2,1,0:T(8,128)} %disp_ref.1, f32[2,8,1024]{2,1,0:T(8,128)} %vel_ref.1, s32[4,8,1024]{2,1,0:T(8,128)} %bonds_ref.1), custom_call_target="tpu_custom_call" | custom-call | tf_op jit(solution)/shard_map/pallas_call | solution.py:396
  22.7 0.6 %copy.7 = f32[2,8,1024]{2,1,0:T(8,128)} copy(f32[2,8,1024]{2,1,0:T(8,128)S(1)} %get-tuple-element.4) | data formatting | bytes 131072
  23.3 0.6 %copy.8 = f32[2,8,1024]{2,1,0:T(8,128)} copy(f32[2,8,1024]{2,1,0:T(8,128)S(1)} %get-tuple-element.5) | data formatting | bytes 131072

commit v5 on v4

--- a/solution.py
+++ b/solution.py
@@ -45,7 +45,7 @@
 
 
 def kernel(
-    disp_ref, vel_ref, bonds_ref, disp_out, vel_out,
+    disp_ref, vel_ref, bonds_ref, disp_out, half_out, accel_out,
     given, given_bonds, state, far, half, packed, masks, total, bond_rows, edge_out, edges_out,
     corner_out, corners_out, rows_in, row_bonds_in, edge_in, corner_in, rows_next, edges_next,
     corners_next, load, send, recv,
@@ -257,6 +257,7 @@
             kick = (0.5 * TIME_STEP) * sums[f]
             value = (near[2 + f] + kick) + kick * again
             half[phase, f, pl.ds(top, GROUP)] = value
+            total[f, pl.ds(top, GROUP)] = sums[f]
             for k in range(GROUP):
                 edges_out[phase, 0, f, pl.ds(top + k, 1), :] = value[k, 0:1]
                 edges_out[phase, 1, f, pl.ds(top + k, 1), :] = value[k, segments - 1 : segments]
@@ -314,6 +315,12 @@
                         outer.append(value.astype(jnp.int32))
                     push_masks(r, packed[r], *outer)
 
+        @pl.when(phase == STEPS)
+        def _():
+            for f in range(2):
+                disp_out[f] = far[f, REACH, REACH : REACH + rows].reshape(rows, segments * LANES)
+                half_out[f] = half[STEPS - 1, f].reshape(rows, segments * LANES)
+
         @pl.when(phase > 0)
         def _():
             for c in mid_copies(phase):
@@ -378,8 +385,7 @@
                 c.start()
 
     for f in range(2):
-        disp_out[f] = far[f, REACH, REACH : REACH + rows].reshape(rows, segments * LANES)
-        vel_out[f] = half[STEPS, f].reshape(rows, segments * LANES)
+        accel_out[f] = total[f].reshape(rows, segments * LANES)
     for phase in [None, *range(1, STEPS + 1)]:
         for c in mid_copies(phase) + rest_copies(phase):
             c.wait_send()
@@ -392,12 +398,11 @@
     vmem = lambda *shape: pltpu.VMEM(shape, jnp.float32)
     bond_slots = REACH * (REACH + 1) // 2
     spec = pl.BlockSpec(memory_space=pltpu.VMEM)
-    results = (jax.ShapeDtypeStruct(disp.shape, disp.dtype),) * 2
-    return pl.pallas_call(
+    earlier, half, accel = pl.pallas_call(
         kernel,
-        out_shape=results,
+        out_shape=(jax.ShapeDtypeStruct(disp.shape, disp.dtype),) * 3,
         in_specs=[pl.BlockSpec(memory_space=pltpu.HBM)] * 3,
-        out_specs=(spec,) * 2,
+        out_specs=(spec,) * 3,
         scratch_shapes=[
             vmem(4, rows, columns),
             pltpu.VMEM((4, rows, columns), jnp.int32),
@@ -424,9 +429,10 @@
             pltpu.SemaphoreType.DMA((STEPS + 1, 9)),
         ],
         compiler_params=pltpu.CompilerParams(
-            collective_id=0, has_side_effects=True, vmem_limit_bytes=55104 * 1024
+            collective_id=0, has_side_effects=True, vmem_limit_bytes=55040 * 1024
         ),
     )(disp, vel, bonds)
+    return earlier + TIME_STEP * half, half + 0.5 * TIME_STEP * accel
 
 
 def solution(mesh):

time: 24.1 us -> 23.5 us (0.975)
  local copies, waits for them, and re-layouts: 1.26 us -> 0 us
  other arithmetic: 0 us -> 0.67 us
    unnamed x2 -> x0, local copies, waits for them, and re-layouts: 1.26 us -> none
    add x0 -> x1, other arithmetic: none -> 0.67 us  [per_device(): return (earlier + TIME_STEP * half, half + 0.5 * TIME_STEP * accel)]
where the time goes in v5:
time: 23.5 us; the launch traced here: 23.3 us
  Pallas kernels  22 us (94%)
  other arithmetic  0.67 us (3%)
  between operations  0.64 us (3%)
    pallas_call x1, Pallas kernels, per_device(): pl.pallas_call(kernel, out_shape=(jax.ShapeDtypeStruct(disp.shape, disp.d...  22 us
    add x1, other arithmetic, per_device(): return (earlier + TIME_STEP * half, half + 0.5 * TIME_STEP * accel)  0.67 us

profile of v5, /device:TPU:1, one launch (start us, length us, event | category | flops | bytes accessed | tf_op | source)
XLA Modules:
  0.0 23.3 jit_solution(13418837634784275560)
XLA Ops:
  0.6 22.0 %shard_map.50 = (f32[2,8,1024]{2,1,0:T(8,128)S(1)}, f32[2,8,1024]{2,1,0:T(8,128)S(1)}, f32[2,8,1024]{2,1,0:T(8,128)S(1)}) custom-call(f32[2,8,1024]{2,1,0:T(8,128)} %disp_ref.1, f32[2,8,1024]{2,1,0:T(8,128)} %vel_ref.1, s32[4,8,1024]{2,1,0:T(8,128)} %bonds_ref.1), custom_call_target="tpu_custom_call" | custom-call | tf_op jit(solution)/shard_map/pallas_call | solution.py:401
  22.6 0.7 %multiply_add_fusion = (f32[2,8,1024]{2,1,0:T(8,128)}, f32[2,8,1024]{2,1,0:T(8,128)}) fusion(f32[2,8,1024]{2,1,0:T(8,128)S(1)} %get-tuple-element.6, f32[2,8,1024]{2,1,0:T(8,128)S(1)} %get-tuple-element.7, f32[2,8,1024]{2,1,0:T(8,128)S(1)} %get-tuple-element.5), kind=kLoop, calls=%fused_computation | loop fusion | flops 65536 | bytes 327680 | tf_op jit(solution)/shard_map/add | solution.py:435

commit v6 on v5

--- a/solution.py
+++ b/solution.py
@@ -54,7 +54,6 @@
     segments = disp_ref.shape[2] // LANES
     groups = rows // GROUP
     assert rows % GROUP == 0 and groups >= 4
-    corner_rows = corner_out.shape[2]
     corner_state = 16
     loads = [
         pltpu.make_async_copy(disp_ref, given.at[0:2], load.at[0]),
@@ -102,15 +101,13 @@
             phase, 3 + side, edges_out.at[phase - 1, side], edges_next.at[phase - 1, 1 - side], gx, y
         )
 
-    def corner_copy(phase, along, across, first_rows=0):
+    def corner_copy(phase, along, across):
         x = lax.rem(gx + nx - 1 + 2 * along, nx)
         y = gy_at[2 * across - 1]
         index = 5 + 2 * along + across
         if phase is None:
-            part = pl.ds(0, first_rows)
             return remote(
-                0, index, corner_out.at[along, across, part],
-                corner_in.at[1 - along, 1 - across, part], x, y,
+                0, index, corner_out.at[along, across], corner_in.at[1 - along, 1 - across], x, y
             )
         return remote(
             phase, index, corners_out.at[phase - 1, along, across],
@@ -125,8 +122,7 @@
         if phase is None:
             out.append(bond_copy())
         return out + [
-            corner_copy(phase, along, across, (corner_state, corner_rows)[along])
-            for along in (0, 1) for across in (0, 1)
+            corner_copy(phase, along, across) for along in (0, 1) for across in (0, 1)
         ]
 
     def by_segments(block):
@@ -271,6 +267,47 @@
 
         @pl.loop(0, 2)
         def _(side):
+            @pl.when(phase == 0)
+            def _():
+                row_copy(None, 1 - side).wait_recv()
+                for across in (0, 1):
+                    corner_copy(None, 1 - side, across).wait_recv()
+                for k in range(REACH):
+                    place_first(
+                        side * (rows + REACH) - REACH + k, lambda plane: rows_in[side, plane, k],
+                        lambda across, plane: corner_in[
+                            side, across, plane * REACH + k : plane * REACH + k + 1, :
+                        ],
+                    )
+
+            @pl.when(jnp.logical_and(phase == 0, side == 0))
+            def _():
+                bond_copy().wait_recv()
+                for r in range(-REACH, 0):
+                    word = jnp.zeros((segments, LANES), jnp.float32)
+                    outer = [jnp.zeros((1, LANES), jnp.float32) for across in (0, 1)]
+                    for a in range(-r, REACH + 1):
+                        slot = row_bond_slots[(a, r)]
+                        at = corner_state + slot
+                        word = word + row_bonds_in[slot] * PACK[a]
+                        for across in (0, 1):
+                            outer[across] += corner_in[0, across, at : at + 1, :] * PACK[a]
+                    push_masks(r, word.astype(jnp.int32), *[x.astype(jnp.int32) for x in outer])
+
+            @pl.when(phase > 0)
+            def _():
+                row_copy(phase, 1 - side).wait_recv()
+                for across in (0, 1):
+                    corner_copy(phase, 1 - side, across).wait_recv()
+                for k in range(REACH):
+                    place_next(
+                        side * (rows + REACH) - REACH + k,
+                        lambda plane: rows_next[phase - 1, side, plane, k],
+                        lambda across, plane: corners_next[
+                            phase - 1, side, across, plane * REACH + k : plane * REACH + k + 1, :
+                        ],
+                    )
+
             sign = 1 - 2 * side
             for depth, sizes in ((0, (-1, -2, -3)), (1, (-3,))):
                 top = depth * GROUP + side * (rows - (2 * depth + 1) * GROUP)
@@ -336,46 +373,6 @@
                     )
 
         inner_forces()
-
-        @pl.when(phase == 0)
-        def _():
-            for c in rest_copies(None):
-                c.wait_recv()
-
-            for along in (0, 1):
-                for k in range(REACH):
-                    place_first(
-                        along * (rows + REACH) - REACH + k, lambda plane: rows_in[along, plane, k],
-                        lambda side, plane: corner_in[
-                            along, side, plane * REACH + k : plane * REACH + k + 1, :
-                        ],
-                    )
-
-            for r in range(-REACH, 0):
-                word = jnp.zeros((segments, LANES), jnp.float32)
-                outer = [jnp.zeros((1, LANES), jnp.float32) for side in (0, 1)]
-                for a in range(-r, REACH + 1):
-                    slot = row_bond_slots[(a, r)]
-                    at = corner_state + slot
-                    word = word + row_bonds_in[slot] * PACK[a]
-                    for side in (0, 1):
-                        outer[side] += corner_in[0, side, at : at + 1, :] * PACK[a]
-                push_masks(r, word.astype(jnp.int32), *[x.astype(jnp.int32) for x in outer])
-
-        @pl.when(phase > 0)
-        def _():
-            for c in rest_copies(phase):
-                c.wait_recv()
-
-            for along in (0, 1):
-                for k in range(REACH):
-                    place_next(
-                        along * (rows + REACH) - REACH + k,
-                        lambda plane: rows_next[phase - 1, along, plane, k],
-                        lambda side, plane: corners_next[
-                            phase - 1, along, side, plane * REACH + k : plane * REACH + k + 1, :
-                        ],
-                    )
 
         outer_forces(phase)
 

time: 23.5 us -> 23.5 us (level)
  no operation moved by 1% of the time
where the time goes in v6:
time: 23.5 us; the launch traced here: 23.4 us
  Pallas kernels  22.1 us (94%)
  other arithmetic  0.67 us (3%)
  between operations  0.64 us (3%)
    pallas_call x1, Pallas kernels, per_device(): pl.pallas_call(kernel, out_shape=(jax.ShapeDtypeStruct(disp.shape, disp.d...  22.1 us
    add x1, other arithmetic, per_device(): return (earlier + TIME_STEP * half, half + 0.5 * TIME_STEP * accel)  0.67 us

profile of v6, /device:TPU:1, one launch (start us, length us, event | category | flops | bytes accessed | tf_op | source)
XLA Modules:
  0.0 23.4 jit_solution(16434586946720338898)
XLA Ops:
  0.6 22.1 %shard_map.50 = (f32[2,8,1024]{2,1,0:T(8,128)S(1)}, f32[2,8,1024]{2,1,0:T(8,128)S(1)}, f32[2,8,1024]{2,1,0:T(8,128)S(1)}) custom-call(f32[2,8,1024]{2,1,0:T(8,128)} %disp_ref.1, f32[2,8,1024]{2,1,0:T(8,128)} %vel_ref.1, s32[4,8,1024]{2,1,0:T(8,128)} %bonds_ref.1), custom_call_target="tpu_custom_call" | custom-call | tf_op jit(solution)/shard_map/pallas_call | solution.py:398
  22.7 0.7 %multiply_add_fusion = (f32[2,8,1024]{2,1,0:T(8,128)}, f32[2,8,1024]{2,1,0:T(8,128)}) fusion(f32[2,8,1024]{2,1,0:T(8,128)S(1)} %get-tuple-element.6, f32[2,8,1024]{2,1,0:T(8,128)S(1)} %get-tuple-element.7, f32[2,8,1024]{2,1,0:T(8,128)S(1)} %get-tuple-element.5), kind=kLoop, calls=%fused_computation | loop fusion | flops 65536 | bytes 327680 | tf_op jit(solution)/shard_map/add | solution.py:432

commit v7 on v5

--- a/solution.py
+++ b/solution.py
@@ -163,7 +163,7 @@
             row_bond_slots[(a, r - rows)] = slot
             slot += 1
     pl.semaphore_wait(barrier, len(around))
-    for c in rest_copies(None) + mid_copies(None):
+    for c in mid_copies(None) + rest_copies(None):
         c.start()
     own_packed = words[0] * PACK[0] + words[1] * PACK[1] + words[2] * PACK[2] + words[3] * PACK[3]
     packed[...] = own_packed.astype(jnp.int32)
@@ -279,19 +279,6 @@
                 signed = [(sign * a, abs(a)) for a in sizes]
                 kicked(phase, top, near, evaluate(near, top, signed, sums))
 
-            @pl.when(phase < STEPS)
-            def _():
-                row_copy(phase + 1, side).start()
-                for f in range(2):
-                    for k in range(REACH):
-                        r = side * (rows - REACH) + k
-                        for across in (0, 1):
-                            corners_out[phase, side, across, f * REACH + k : f * REACH + k + 1, :] = (
-                                edges_out[phase, across, f, pl.ds(r, 1), :]
-                            )
-                for across in (0, 1):
-                    corner_copy(phase + 1, side, across).start()
-
     @pl.loop(0, STEPS + 1)
     def _(phase):
         @pl.when(phase == 0)
@@ -299,10 +286,10 @@
             for c in mid_copies(None):
                 c.wait_recv()
 
-            @pl.loop(0, groups)
+            @pl.loop(0, groups // 2)
             def _(group):
-                for k in range(GROUP):
-                    r = group * GROUP + k
+                for k in range(2 * GROUP):
+                    r = group * (2 * GROUP) + k
                     place_first(
                         r, lambda plane: state[plane, r],
                         lambda side, plane: edge_in[side, plane, pl.ds(r, 1), :],
@@ -326,14 +313,11 @@
             for c in mid_copies(phase):
                 c.wait_recv()
 
-            @pl.loop(0, groups // 2)
-            def _(group):
-                for k in range(2 * GROUP):
-                    r = group * (2 * GROUP) + k
-                    place_next(
-                        r, lambda plane: half[phase - 1, plane, r],
-                        lambda side, plane: edges_next[phase - 1, side, plane, pl.ds(r, 1), :],
-                    )
+            for r in range(rows):
+                place_next(
+                    r, lambda plane: half[phase - 1, plane, r],
+                    lambda side, plane: edges_next[phase - 1, side, plane, r : r + 1, :],
+                )
 
         inner_forces()
 
@@ -381,8 +365,16 @@
 
         @pl.when(phase < STEPS)
         def _():
-            for c in mid_copies(phase + 1):
+            for c in mid_copies(phase + 1) + [row_copy(phase + 1, side) for side in (0, 1)]:
                 c.start()
+            for along in (0, 1):
+                for across in (0, 1):
+                    for f in range(2):
+                        r = along * (rows - REACH)
+                        corners_out[phase, along, across, f * REACH : (f + 1) * REACH, :] = (
+                            edges_out[phase, across, f, r : r + REACH, :]
+                        )
+                    corner_copy(phase + 1, along, across).start()
 
     for f in range(2):
         accel_out[f] = total[f].reshape(rows, segments * LANES)

time: 23.5 us -> 23.3 us (level)
  no operation moved by 1% of the time
where the time goes in v7:
time: 23.3 us; the launch traced here: 23.1 us
  Pallas kernels  21.8 us (94%)
  other arithmetic  0.67 us (3%)
  between operations  0.64 us (3%)
    pallas_call x1, Pallas kernels, per_device(): pl.pallas_call(kernel, out_shape=(jax.ShapeDtypeStruct(disp.shape, disp.d...  21.8 us
    add x1, other arithmetic, per_device(): return (earlier + TIME_STEP * half, half + 0.5 * TIME_STEP * accel)  0.67 us

profile of v7, /device:TPU:1, one launch (start us, length us, event | category | flops | bytes accessed | tf_op | source)
XLA Modules:
  0.0 23.1 jit_solution(4522792774975463878)
XLA Ops:
  0.6 21.8 %shard_map.50 = (f32[2,8,1024]{2,1,0:T(8,128)S(1)}, f32[2,8,1024]{2,1,0:T(8,128)S(1)}, f32[2,8,1024]{2,1,0:T(8,128)S(1)}) custom-call(f32[2,8,1024]{2,1,0:T(8,128)} %disp_ref.1, f32[2,8,1024]{2,1,0:T(8,128)} %vel_ref.1, s32[4,8,1024]{2,1,0:T(8,128)} %bonds_ref.1), custom_call_target="tpu_custom_call" | custom-call | tf_op jit(solution)/shard_map/pallas_call | solution.py:393
  22.5 0.7 %multiply_add_fusion = (f32[2,8,1024]{2,1,0:T(8,128)}, f32[2,8,1024]{2,1,0:T(8,128)}) fusion(f32[2,8,1024]{2,1,0:T(8,128)S(1)} %get-tuple-element.6, f32[2,8,1024]{2,1,0:T(8,128)S(1)} %get-tuple-element.7, f32[2,8,1024]{2,1,0:T(8,128)S(1)} %get-tuple-element.5), kind=kLoop, calls=%fused_computation | loop fusion | flops 65536 | bytes 327680 | tf_op jit(solution)/shard_map/add | solution.py:427

commit v8 on v7

--- a/solution.py
+++ b/solution.py
@@ -206,7 +206,7 @@
     def evaluate(near, top, signed, sums):
         force_x, force_y = sums
         for a, size in signed:
-            near_x = near[0] - lax.convert_element_type(a, jnp.float32)
+            near_x = near[0] - float(a)
             at = pl.ds(top + REACH + a, GROUP)
             for b in SHIFTS:
                 if size == 0 and b == 0:
@@ -233,8 +233,7 @@
     zero = jnp.zeros((GROUP, segments, LANES), jnp.float32)
 
     def inner_forces():
-        @pl.loop(0, 2)
-        def _(side):
+        for side in (0, 1):
             sign = 1 - 2 * side
             for depth, sizes in ((0, range(0, REACH + 1)), (1, range(-2, REACH + 1))):
                 top = depth * GROUP + side * (rows - (2 * depth + 1) * GROUP)
@@ -269,8 +268,7 @@
                 top = group * GROUP
                 kicked(phase, top, near_of(top), [total[f, pl.ds(top, GROUP)] for f in range(2)])
 
-        @pl.loop(0, 2)
-        def _(side):
+        for side in (0, 1):
             sign = 1 - 2 * side
             for depth, sizes in ((0, (-1, -2, -3)), (1, (-3,))):
                 top = depth * GROUP + side * (rows - (2 * depth + 1) * GROUP)

time: 23.3 us -> 23.3 us (level)
  no operation moved by 1% of the time
where the time goes in v8:
time: 23.3 us; the launch traced here: 23.1 us
  Pallas kernels  21.8 us (94%)
  other arithmetic  0.67 us (3%)
  between operations  0.64 us (3%)
    pallas_call x1, Pallas kernels, per_device(): pl.pallas_call(kernel, out_shape=(jax.ShapeDtypeStruct(disp.shape, disp.d...  21.8 us
    add x1, other arithmetic, per_device(): return (earlier + TIME_STEP * half, half + 0.5 * TIME_STEP * accel)  0.67 us

profile of v8, /device:TPU:1, one launch (start us, length us, event | category | flops | bytes accessed | tf_op | source)
XLA Modules:
  0.0 23.1 jit_solution(17561305903849092882)
XLA Ops:
  0.6 21.8 %shard_map.50 = (f32[2,8,1024]{2,1,0:T(8,128)S(1)}, f32[2,8,1024]{2,1,0:T(8,128)S(1)}, f32[2,8,1024]{2,1,0:T(8,128)S(1)}) custom-call(f32[2,8,1024]{2,1,0:T(8,128)} %disp_ref.1, f32[2,8,1024]{2,1,0:T(8,128)} %vel_ref.1, s32[4,8,1024]{2,1,0:T(8,128)} %bonds_ref.1), custom_call_target="tpu_custom_call" | custom-call | tf_op jit(solution)/shard_map/pallas_call | solution.py:391
  22.4 0.7 %multiply_add_fusion = (f32[2,8,1024]{2,1,0:T(8,128)}, f32[2,8,1024]{2,1,0:T(8,128)}) fusion(f32[2,8,1024]{2,1,0:T(8,128)S(1)} %get-tuple-element.6, f32[2,8,1024]{2,1,0:T(8,128)S(1)} %get-tuple-element.7, f32[2,8,1024]{2,1,0:T(8,128)S(1)} %get-tuple-element.5), kind=kLoop, calls=%fused_computation | loop fusion | flops 65536 | bytes 327680 | tf_op jit(solution)/shard_map/add | solution.py:425

commit v9 on v8

--- a/solution.py
+++ b/solution.py
@@ -261,6 +261,49 @@
                 edges_out[phase, 0, f, pl.ds(top + k, 1), :] = value[k, 0:1]
                 edges_out[phase, 1, f, pl.ds(top + k, 1), :] = value[k, segments - 1 : segments]
 
+    def arrive(phase, side):
+        first = side * (rows + REACH) - REACH
+
+        @pl.when(phase == 0)
+        def _():
+            row_copy(None, 1 - side).wait_recv()
+            for across in (0, 1):
+                corner_copy(
+                    None, 1 - side, across, (corner_state, corner_rows)[1 - side]
+                ).wait_recv()
+            for k in range(REACH):
+                place_first(
+                    first + k, lambda plane: rows_in[side, plane, k],
+                    lambda across, plane: corner_in[
+                        side, across, plane * REACH + k : plane * REACH + k + 1, :
+                    ],
+                )
+            if side == 0:
+                bond_copy().wait_recv()
+                for r in range(-REACH, 0):
+                    word = jnp.zeros((segments, LANES), jnp.float32)
+                    outer = [jnp.zeros((1, LANES), jnp.float32) for across in (0, 1)]
+                    for a in range(-r, REACH + 1):
+                        slot = row_bond_slots[(a, r)]
+                        at = corner_state + slot
+                        word = word + row_bonds_in[slot] * PACK[a]
+                        for across in (0, 1):
+                            outer[across] += corner_in[0, across, at : at + 1, :] * PACK[a]
+                    push_masks(r, word.astype(jnp.int32), *[x.astype(jnp.int32) for x in outer])
+
+        @pl.when(phase > 0)
+        def _():
+            row_copy(phase, 1 - side).wait_recv()
+            for across in (0, 1):
+                corner_copy(phase, 1 - side, across).wait_recv()
+            for k in range(REACH):
+                place_next(
+                    first + k, lambda plane: rows_next[phase - 1, side, plane, k],
+                    lambda across, plane: corners_next[
+                        phase - 1, side, across, plane * REACH + k : plane * REACH + k + 1, :
+                    ],
+                )
+
     def outer_forces(phase):
         if groups > 4:
             @pl.loop(2, groups - 2)
@@ -269,6 +312,7 @@
                 kicked(phase, top, near_of(top), [total[f, pl.ds(top, GROUP)] for f in range(2)])
 
         for side in (0, 1):
+            arrive(phase, side)
             sign = 1 - 2 * side
             for depth, sizes in ((0, (-1, -2, -3)), (1, (-3,))):
                 top = depth * GROUP + side * (rows - (2 * depth + 1) * GROUP)
@@ -276,6 +320,10 @@
                 sums = [total[f, pl.ds(top, GROUP)] for f in range(2)]
                 signed = [(sign * a, abs(a)) for a in sizes]
                 kicked(phase, top, near, evaluate(near, top, signed, sums))
+            if side == 0:
+                @pl.when(phase < STEPS)
+                def _():
+                    row_copy(phase + 1, 0).start()
 
     @pl.loop(0, STEPS + 1)
     def _(phase):
@@ -319,51 +367,11 @@
 
         inner_forces()
 
-        @pl.when(phase == 0)
-        def _():
-            for c in rest_copies(None):
-                c.wait_recv()
-
-            for along in (0, 1):
-                for k in range(REACH):
-                    place_first(
-                        along * (rows + REACH) - REACH + k, lambda plane: rows_in[along, plane, k],
-                        lambda side, plane: corner_in[
-                            along, side, plane * REACH + k : plane * REACH + k + 1, :
-                        ],
-                    )
-
-            for r in range(-REACH, 0):
-                word = jnp.zeros((segments, LANES), jnp.float32)
-                outer = [jnp.zeros((1, LANES), jnp.float32) for side in (0, 1)]
-                for a in range(-r, REACH + 1):
-                    slot = row_bond_slots[(a, r)]
-                    at = corner_state + slot
-                    word = word + row_bonds_in[slot] * PACK[a]
-                    for side in (0, 1):
-                        outer[side] += corner_in[0, side, at : at + 1, :] * PACK[a]
-                push_masks(r, word.astype(jnp.int32), *[x.astype(jnp.int32) for x in outer])
-
-        @pl.when(phase > 0)
-        def _():
-            for c in rest_copies(phase):
-                c.wait_recv()
-
-            for along in (0, 1):
-                for k in range(REACH):
-                    place_next(
-                        along * (rows + REACH) - REACH + k,
-                        lambda plane: rows_next[phase - 1, along, plane, k],
-                        lambda side, plane: corners_next[
-                            phase - 1, along, side, plane * REACH + k : plane * REACH + k + 1, :
-                        ],
-                    )
-
         outer_forces(phase)
 
         @pl.when(phase < STEPS)
         def _():
-            for c in mid_copies(phase + 1) + [row_copy(phase + 1, side) for side in (0, 1)]:
+            for c in mid_copies(phase + 1) + [row_copy(phase + 1, 1)]:
                 c.start()
             for along in (0, 1):
                 for across in (0, 1):

time: 23.3 us -> 23.2 us (level)
  no operation moved by 1% of the time
where the time goes in v9:
time: 23.2 us; the launch traced here: 23 us
  Pallas kernels  21.7 us (94%)
  other arithmetic  0.67 us (3%)
  between operations  0.64 us (3%)
    pallas_call x1, Pallas kernels, per_device(): pl.pallas_call(kernel, out_shape=(jax.ShapeDtypeStruct(disp.shape, disp.d...  21.7 us
    add x1, other arithmetic, per_device(): return (earlier + TIME_STEP * half, half + 0.5 * TIME_STEP * accel)  0.67 us

profile of v9, /device:TPU:1, one launch (start us, length us, event | category | flops | bytes accessed | tf_op | source)
XLA Modules:
  0.0 23.0 jit_solution(11896890589550563822)
XLA Ops:
  0.6 21.7 %shard_map.50 = (f32[2,8,1024]{2,1,0:T(8,128)S(1)}, f32[2,8,1024]{2,1,0:T(8,128)S(1)}, f32[2,8,1024]{2,1,0:T(8,128)S(1)}) custom-call(f32[2,8,1024]{2,1,0:T(8,128)} %disp_ref.1, f32[2,8,1024]{2,1,0:T(8,128)} %vel_ref.1, s32[4,8,1024]{2,1,0:T(8,128)} %bonds_ref.1), custom_call_target="tpu_custom_call" | custom-call | tf_op jit(solution)/shard_map/pallas_call | solution.py:399
  22.3 0.7 %multiply_add_fusion = (f32[2,8,1024]{2,1,0:T(8,128)}, f32[2,8,1024]{2,1,0:T(8,128)}) fusion(f32[2,8,1024]{2,1,0:T(8,128)S(1)} %get-tuple-element.6, f32[2,8,1024]{2,1,0:T(8,128)S(1)} %get-tuple-element.7, f32[2,8,1024]{2,1,0:T(8,128)S(1)} %get-tuple-element.5), kind=kLoop, calls=%fused_computation | loop fusion | flops 65536 | bytes 327680 | tf_op jit(solution)/shard_map/add | solution.py:433

commit v10 on v9

--- a/solution.py
+++ b/solution.py
@@ -145,6 +145,9 @@
             at = slice(plane * REACH, (plane + 1) * REACH)
             corner_out[along, 0, at] = block[top : top + REACH, 0:LANES]
             corner_out[along, 1, at] = block[top : top + REACH, last : last + LANES]
+    pl.semaphore_wait(barrier, len(around))
+    for side in (0, 1):
+        row_copy(None, side).start()
     loads[2].wait()
     words = []
     for w in range(4):
@@ -162,8 +165,7 @@
                 corner_out[1, across, at : at + 1] = edge_out[across, 4 + a, r : r + 1]
             row_bond_slots[(a, r - rows)] = slot
             slot += 1
-    pl.semaphore_wait(barrier, len(around))
-    for c in mid_copies(None) + rest_copies(None):
+    for c in mid_copies(None) + rest_copies(None)[2:]:
         c.start()
     own_packed = words[0] * PACK[0] + words[1] * PACK[1] + words[2] * PACK[2] + words[3] * PACK[3]
     packed[...] = own_packed.astype(jnp.int32)

time: 23.2 us -> 23.2 us (level)
  no operation moved by 1% of the time
where the time goes in v10:
time: 23.2 us; the launch traced here: 23 us
  Pallas kernels  21.7 us (94%)
  other arithmetic  0.67 us (3%)
  between operations  0.64 us (3%)
    pallas_call x1, Pallas kernels, per_device(): pl.pallas_call(kernel, out_shape=(jax.ShapeDtypeStruct(disp.shape, disp.d...  21.7 us
    add x1, other arithmetic, per_device(): return (earlier + TIME_STEP * half, half + 0.5 * TIME_STEP * accel)  0.67 us

profile of v10, /device:TPU:1, one launch (start us, length us, event | category | flops | bytes accessed | tf_op | source)
XLA Modules:
  0.0 23.0 jit_solution(16728644649792766634)
XLA Ops:
  0.6 21.7 %shard_map.50 = (f32[2,8,1024]{2,1,0:T(8,128)S(1)}, f32[2,8,1024]{2,1,0:T(8,128)S(1)}, f32[2,8,1024]{2,1,0:T(8,128)S(1)}) custom-call(f32[2,8,1024]{2,1,0:T(8,128)} %disp_ref.1, f32[2,8,1024]{2,1,0:T(8,128)} %vel_ref.1, s32[4,8,1024]{2,1,0:T(8,128)} %bonds_ref.1), custom_call_target="tpu_custom_call" | custom-call | tf_op jit(solution)/shard_map/pallas_call | solution.py:401
  22.3 0.7 %multiply_add_fusion = (f32[2,8,1024]{2,1,0:T(8,128)}, f32[2,8,1024]{2,1,0:T(8,128)}) fusion(f32[2,8,1024]{2,1,0:T(8,128)S(1)} %get-tuple-element.6, f32[2,8,1024]{2,1,0:T(8,128)S(1)} %get-tuple-element.7, f32[2,8,1024]{2,1,0:T(8,128)S(1)} %get-tuple-element.5), kind=kLoop, calls=%fused_computation | loop fusion | flops 65536 | bytes 327680 | tf_op jit(solution)/shard_map/add | solution.py:435
